TPU v7x, 256 devices: a whole 4x4x8 slice. The times are simulated.
256 devices in a mesh: wide: 32 (over x, z), narrow: 8 (over y, core).
Axes of the slice: x: 4, y: 4, z: 8, core: 2. Of those that a mesh axis runs over, the one named last changes fastest.
Arguments:
- embeddings: bfloat16 [131072, 1024], P('wide', 'narrow')
- centroids: bfloat16 [262144, 1024], P('wide', 'narrow')
- level2_cluster_index: int32 [512], P('wide'), may hold values from 0 to 16383, as said below
- child_lists: int32 [16384, 128], P('wide'), may hold values from 0 to 262143, as said below
Outputs:
- new_centroids: float32 [262144, 1024], P('wide', 'narrow')
Inputs may be any that keep to these rules, and one draw needn't show every extreme that they name: `level2_cluster_index`: Level-2 cluster g belongs to group g // 512. Among the 16 blocks of one index of wide, at most 2 belong to clusters of one group. `child_lists`: the children of cluster g lie in (g // 512) * 8192 to (g // 512 + 1) * 8192 - 1; a list may name a centroid more than once.
All inputs are finite; a program needn't handle non-finite values.
Results may differ from a plain program's by a relative error of at most 0.0014.
Values may be sent and summed in bfloat16 or wider, within the bound.
A program may use at most 128 MiB of HBM per device.

v0:
```python
import math

import jax
import jax.numpy as jnp
from jax import lax
from jax.sharding import PartitionSpec as P

D = 1024


def slot_layout(level2_cluster_index, groups_owned, owners, capacity):
    blocks = level2_cluster_index.shape[0]
    owner_of_block = level2_cluster_index // groups_owned
    onehot = (owner_of_block[:, None] == jnp.arange(owners, dtype=jnp.int32)[None, :]).astype(
        jnp.int32
    )
    position = jnp.sum((jnp.cumsum(onehot, axis=0) - onehot) * onehot, axis=1)
    slot_of_block = owner_of_block * capacity + position
    matches = slot_of_block[None, :] == jnp.arange(owners * capacity, dtype=jnp.int32)[:, None]
    filled = jnp.any(matches, axis=1)
    block_of_slot = jnp.sum(
        jnp.where(matches, jnp.arange(blocks, dtype=jnp.int32)[None, :], 0), axis=1
    )
    return (slot_of_block, block_of_slot, filled)


def weigh(row_block_groups, embedding_table):
    dot_products = jnp.einsum(
        "ibw,idw->ibd", row_block_groups, embedding_table, preferred_element_type=jnp.float32
    )
    table_f = embedding_table.astype(jnp.float32)
    lengths = jnp.sum(table_f * table_f, axis=-1)
    partial_score = (2.0 * dot_products - lengths[:, None, :]) * (1.0 / math.sqrt(D))
    total_score = lax.psum(partial_score, "narrow")
    return jax.nn.softmax(total_score, axis=-1).astype(jnp.bfloat16)


def block_partials(soft_weight_matrix, row_block_groups):
    block_weighted_totals = jnp.einsum(
        "gis,gik->gsk", soft_weight_matrix, row_block_groups, preferred_element_type=jnp.float32
    )
    block_counts = jnp.sum(soft_weight_matrix.astype(jnp.float32), axis=1)
    return (block_weighted_totals, block_counts)


def body(embeddings, centroids, level2_cluster_index, child_lists):
    owners = lax.axis_size("wide")
    here_index = lax.axis_index("wide")
    blocks = level2_cluster_index.shape[0]
    block_rows = embeddings.shape[0] // blocks
    feature_matrix = embeddings.shape[1]
    kids_count = child_lists.shape[1]
    groups_owned = child_lists.shape[0]
    centres_owned = centroids.shape[0]
    capacity = max(2, 3 * blocks // owners)
    slots = owners * capacity
    row_block_groups = embeddings.reshape(blocks, block_rows, feature_matrix)
    slot_of_block, block_of_slot, filled = slot_layout(
        level2_cluster_index, groups_owned, owners, capacity
    )
    slot_ids = jnp.where(filled, level2_cluster_index[block_of_slot], -1).reshape(owners, capacity)
    incoming_ids = lax.all_to_all(slot_ids, "wide", split_axis=0, concat_axis=0, tiled=True)
    local_cluster = jnp.clip(incoming_ids - here_index * groups_owned, 0, groups_owned - 1)
    children = (child_lists[local_cluster] - here_index * centres_owned).reshape(slots, kids_count)
    rows_out = centroids[children].reshape(owners, capacity, kids_count, feature_matrix)
    input_rows = lax.all_to_all(rows_out, "wide", split_axis=0, concat_axis=0, tiled=True)
    embedding_table = input_rows.reshape(slots, kids_count, feature_matrix)[slot_of_block]
    soft_weight_matrix = weigh(row_block_groups, embedding_table)
    block_weighted_totals, block_counts = block_partials(soft_weight_matrix, row_block_groups)
    sums_slots = (
        jnp.zeros((slots, kids_count, feature_matrix), jnp.float32)
        .at[slot_of_block]
        .set(block_weighted_totals)
    )
    counts_slots = jnp.zeros((slots, kids_count), jnp.float32).at[slot_of_block].set(block_counts)
    sums_back, counts_back = (
        lax.all_to_all(
            sums_slots.reshape(owners, capacity, kids_count, feature_matrix),
            "wide",
            split_axis=0,
            concat_axis=0,
            tiled=True,
        ),
        lax.all_to_all(
            counts_slots.reshape(owners, capacity, kids_count),
            "wide",
            split_axis=0,
            concat_axis=0,
            tiled=True,
        ),
    )
    slot_sums = sums_back.reshape(slots * kids_count, feature_matrix)
    slot_counts = counts_back.reshape(slots * kids_count)
    flat_children = children.reshape(-1)
    sums = jax.ops.segment_sum(slot_sums, flat_children, num_segments=centres_owned)
    counts = jax.ops.segment_sum(slot_counts, flat_children, num_segments=centres_owned)
    return (sums + centroids.astype(jnp.float32)) / (counts + 1.0)[:, None]


def solution(mesh):
    placed = (P("wide", "narrow"), P("wide", "narrow"), P("wide"), P("wide", None))
    return jax.shard_map(
        body, mesh=mesh, in_specs=placed, out_specs=P("wide", "narrow"), check_vma=False
    )
```

profile of v0, /device:TPU:95, one launch (start us, length us, event | category | flops | bytes accessed | tf_op | source)
XLA Modules:
  0.0 367.8 jit_solution(11430012546903273824)
XLA Ops:
  6.5 0.8 and_select_fusion
  8.5 1.4 gather_fusion
  9.9 0.7 select_n.63
  10.6 10.1 %all-to-all-start = ((s32[32,1,2]{2,1,0:T(1,128)}), s32[32,1,2]{2,1,0:T(1,128)S(1)}, u32[]{:S(2)}, u32[]{:S(2)}) async-start(s32[32,1,2]{2,1,0:T(1,128)} %bitcast.2), calls=%async_computation | async-start | bytes 32768 | tf_op jit(solution)/shard_map/all_to_all | solution.py:62
  20.8 5.2 %all-to-all-done = s32[32,1,2]{2,1,0:T(1,128)S(1)} async-done(((s32[32,1,2]{2,1,0:T(1,128)}), s32[32,1,2]{2,1,0:T(1,128)S(1)}, u32[]{:S(2)}, u32[]{:S(2)}) %all-to-all-start) | async-done | bytes 288 | tf_op jit(solution)/shard_map/all_to_all | solution.py:62
  26.3 1.5 gather_fusion.1
  27.8 30.1 %gather_fusion.2 = bf16[8192,128]{1,0:T(8,128)(2,1)} fusion(bf16[8192,128]{1,0:T(8,128)(2,1)} %param.5, s32[8192]{0:T(1024)S(1)} %fusion.2), kind=kCustom, calls=%fused_computation.2 | custom fusion | bytes 4227072 | tf_op jit(solution)/shard_map/gather | solution.py:65
  58.0 7.4 %all-to-all-start.1 = ((bf16[32,2,128,128]{3,2,1,0:T(8,128)(2,1)}), bf16[32,2,128,128]{3,2,1,0:T(8,128)(2,1)S(1)}, u32[]{:S(2)}, u32[]{:S(2)}) async-start(bf16[32,2,128,128]{3,2,1,0:T(8,128)(2,1)} %bitcast.7), calls=%async_computation.1 | async-start | bytes 4194304 | tf_op jit(solution)/shard_map/all_to_all | solution.py:66
  65.4 45.3 %all-to-all-done.1 = bf16[32,2,128,128]{3,2,1,0:T(8,128)(2,1)S(1)} async-done(((bf16[32,2,128,128]{3,2,1,0:T(8,128)(2,1)}), bf16[32,2,128,128]{3,2,1,0:T(8,128)(2,1)S(1)}, u32[]{:S(2)}, u32[]{:S(2)}) %all-to-all-start.1) | async-done | bytes 2097184 | tf_op jit(solution)/shard_map/all_to_all | solution.py:66
  110.7 1.3 copy-done.2
  112.0 2.2 gather_fusion.3
  114.7 1.8 multiply_bitcast_fusion
  116.4 72.7 %all-reduce.2.cloned.1.call-done = f32[16,256,128]{1,2,0:T(8,128)} async-done(((f32[16,256,128]{1,2,0:T(8,128)}), f32[16,256,128]{1,2,0:T(8,128)}) %all-reduce.2.cloned.1.call-update) | async-done | bytes 2097168 | tf_op jit(solution)/shard_map/psum | solution.py:34
  189.1 2.6 fusion.10
  192.1 1.2 scatter_custom_fusion.2
  193.3 9.4 %all-to-all-start.3 = ((f32[32,2,128]{2,1,0:T(2,128)}), f32[32,2,128]{2,1,0:T(2,128)S(1)}, u32[]{:S(2)}, u32[]{:S(2)}) async-start(f32[32,2,128]{2,1,0:T(2,128)} %bitcast.13), calls=%async_computation.3 | async-start | bytes 65536 | tf_op jit(solution)/shard_map/all_to_all | solution.py:84
  203.2 2.5 broadcast_in_dim.27
  205.7 3.0 scatter_fusion
  208.7 9.4 %all-to-all-start.2 = ((f32[32,2,128,128]{3,2,1,0:T(8,128)}), f32[32,2,128,128]{3,2,1,0:T(8,128)}, u32[]{:S(2)}, u32[]{:S(2)}) async-start(f32[32,2,128,128]{3,2,1,0:T(8,128)} %bitcast.33), calls=%async_computation.2 | async-start | bytes 8388608 | tf_op jit(solution)/shard_map/all_to_all | solution.py:77
  218.1 2.3 convert_element_type.15
  220.4 43.2 %scatter_custom_fusion.3 = f32[8192]{0:T(1024)S(1)} fusion(s32[8192]{0:T(1024)S(1)} %subtract_bitcast_fusion, f32[8192]{0:T(1024)S(1)} %bitcast.35, f32[]{:T(128)} %constant.60.clone.1), kind=kCustom, calls=%fused_computation.21 | custom fusion | flops 8192 | bytes 32772 | tf_op jit(solution)/shard_map/scatter-add | solution.py:96
  263.6 49.1 %all-to-all-done.2 = f32[32,2,128,128]{3,2,1,0:T(8,128)} async-done(((f32[32,2,128,128]{3,2,1,0:T(8,128)}), f32[32,2,128,128]{3,2,1,0:T(8,128)}, u32[]{:S(2)}, u32[]{:S(2)}) %all-to-all-start.2) | async-done | bytes 4194336 | tf_op jit(solution)/shard_map/all_to_all | solution.py:77
  312.7 44.0 %scatter_fusion.1 = f32[8192,128]{1,0:T(8,128)} fusion(f32[8192,128]{1,0:T(8,128)} %convert_element_type.15, s32[8192]{0:T(1024)S(1)} %subtract_bitcast_fusion, f32[8192,128]{1,0:T(8,128)} %bitcast.12), kind=kCustom, calls=%fused_computation.5 | custom fusion | flops 1048576 | bytes 12615680 | tf_op jit(solution)/shard_map/scatter-add | solution.py:95
  356.7 4.2 %broadcast_divide_fusion = f32[8192,128]{1,0:T(8,128)} fusion(f32[8192,128]{1,0:T(8,128)} %scatter_fusion.1, f32[8192]{0:T(1024)S(1)} %scatter_custom_fusion.3), kind=kLoop, calls=%fused_computation.9 | loop fusion | flops 1048576 | bytes 8421376 | tf_op jit(solution)/shard_map/div | solution.py:97
  (28 shorter events, 2.7 us)
Async XLA Ops:
  6.5 108.1 %copy-start = (bf16[4096,128]{1,0:T(8,128)(2,1)S(1)}, bf16[4096,128]{1,0:T(8,128)(2,1)}, u32[]{:S(2)}) copy-start(bf16[4096,128]{1,0:T(8,128)(2,1)} %param.4) | copy-start | bytes 3145732
  10.6 15.4 %all-to-all-start = ((s32[32,1,2]{2,1,0:T(1,128)}), s32[32,1,2]{2,1,0:T(1,128)S(1)}, u32[]{:S(2)}, u32[]{:S(2)}) async-start(s32[32,1,2]{2,1,0:T(1,128)} %bitcast.2), calls=%async_computation | async-start | bytes 32768 | tf_op jit(solution)/shard_map/all_to_all | solution.py:62
  58.0 52.8 %all-to-all-start.1 = ((bf16[32,2,128,128]{3,2,1,0:T(8,128)(2,1)}), bf16[32,2,128,128]{3,2,1,0:T(8,128)(2,1)S(1)}, u32[]{:S(2)}, u32[]{:S(2)}) async-start(bf16[32,2,128,128]{3,2,1,0:T(8,128)(2,1)} %bitcast.7), calls=%async_computation.1 | async-start | bytes 4194304 | tf_op jit(solution)/shard_map/all_to_all | solution.py:66
  65.3 123.8 %all-reduce.2.cloned.1.call-start = ((), (), s32[]{:S(2)}) async-start(), calls=%async_computation.4 | async-start | bytes 4194304 | tf_op jit(solution)/shard_map/psum | solution.py:34
  110.7 1.3 copy-start.2
  193.3 15.4 %all-to-all-start.3 = ((f32[32,2,128]{2,1,0:T(2,128)}), f32[32,2,128]{2,1,0:T(2,128)S(1)}, u32[]{:S(2)}, u32[]{:S(2)}) async-start(f32[32,2,128]{2,1,0:T(2,128)} %bitcast.13), calls=%async_computation.3 | async-start | bytes 65536 | tf_op jit(solution)/shard_map/all_to_all | solution.py:84
  208.7 9.4 %copy-start.1 = (bf16[8192,128]{1,0:T(8,128)(2,1)S(1)}, bf16[8192,128]{1,0:T(8,128)(2,1)}, u32[]{:S(2)}) copy-start(bf16[8192,128]{1,0:T(8,128)(2,1)} %param.5) | copy-start | bytes 6291460
  208.7 104.0 %all-to-all-start.2 = ((f32[32,2,128,128]{3,2,1,0:T(8,128)}), f32[32,2,128,128]{3,2,1,0:T(8,128)}, u32[]{:S(2)}, u32[]{:S(2)}) async-start(f32[32,2,128,128]{3,2,1,0:T(8,128)} %bitcast.33), calls=%async_computation.2 | async-start | bytes 8388608 | tf_op jit(solution)/shard_map/all_to_all | solution.py:77
Sparse Core Ops, SparseCore 0:
  116.6 72.4 all-reduce.1
where the time goes:
time: 371 us; the launch traced here: 368 us
  waiting for transfers between devices  172 us (46%)
  other arithmetic  99 us (27%)
  local copies, waits for them, and re-layouts  44.3 us (12%)
  starting transfers between devices  36.4 us (10%)
  between operations  13.5 us (4%)
    psum x1, waiting for transfers between devices, weigh(): total_score = lax.psum(partial_score, 'narrow')  72.7 us
    all_to_all x1, waiting for transfers between devices, body(): lax.all_to_all(sums_slots.reshape(owners, capacity, kids_count, feature_m...  49.1 us
    all_to_all x1, waiting for transfers between devices, body(): lax.all_to_all(rows_out, 'wide', split_axis=0, concat_axis=0, tiled=True)  45.3 us
    scatter-add x1, other arithmetic, body(): jax.ops.segment_sum(slot_sums, flat_children, num_segments=centres_owned)  44 us
    scatter-add x1, other arithmetic, body(): jax.ops.segment_sum(slot_counts, flat_children, num_segments=centres_owned)  43.2 us
    gather x1, local copies, waits for them, and re-layouts, body(): centroids[children].reshape(owners, capacity, kids_count, feature_matrix)  30.1 us
    all_to_all x1, starting transfers between devices, body(): lax.all_to_all(slot_ids, 'wide', split_axis=0, concat_axis=0, tiled=True)  10.1 us
    all_to_all x1, starting transfers between devices, body(): lax.all_to_all(counts_slots.reshape(owners, capacity, kids_count), 'wide'...  9.44 us
  transfers between devices with their start and end apart: 5, of which 4 were waited for; matrix products, arithmetic and copies ran while one was open for 14% of the time, Pallas kernels for 0%

commit v1 on v0

v1 whole, which is shorter than its diff:
```python
import functools
import math

import jax
import jax.numpy as jnp
from jax import lax
from jax.experimental import pallas as pl
from jax.experimental.pallas import tpu as pltpu
from jax.sharding import PartitionSpec as P

D = 1024
X, Z = 4, 8
W = X * Z
N = 8
RB = 256
CH = 128
F = 128
BLK = 16
GW = 512
CW = 8192
MESH = pl.DeviceIdType.MESH
NT = (((1,), (1,)), ((), ()))


def shifted(me, dx, dz):
    return lax.rem(me // Z + dx, X) * Z + lax.rem(lax.rem(me, Z) + dz, Z)


def shifted(me, dx, dz):
    return lax.rem(me // Z + dx, X) * Z + lax.rem(lax.rem(me, Z) + dz, Z)


def at_offset(me, k):
    return shifted(me, k // Z, lax.rem(k, Z))


def first_two(mask, lane):
    first = jnp.min(jnp.where(mask, lane, 127), axis=1, keepdims=True)
    rest = mask & (lane != first)
    second = jnp.min(jnp.where(rest, lane, 127), axis=1, keepdims=True)
    return first, second, rest


ROWS = 64
OWN_AT, MINE, PICK, LAST = W, W + 8, W + 16, W + 24


def exchange_kernel(
    ids_ref, child_ref, cent_ref, emb_ref,
    q_out, sc_out, kids_out, tab_out, dup_out, factor_out,
    ids_all, tab_s, kids_s, cent_b, child_v, cent_f, stage, counts_v, x_send,
    hop_send, hop_recv, xfull, csel, ctab, qsend, scs, qrecv, scr, pick, scu, swork,
    local_sem, ids_ss, ids_rs, e_ss, e_rs, d_ss, d_rs, h_ss, h_rs, c_ss, c_rs, s_ss, s_rs,
    t_ss, t_rs, v_ss, v_rs, g_ss, g_rs, u_ss, u_rs, own_sem, *many,
):
    x_recv, rings = many[:Z], (many[Z : Z + 4], many[Z + 4 :] + many[Z + 3 : Z + 4])
    me = lax.axis_index("wide")
    mn = lax.axis_index("narrow")
    mx, mz = me // Z, lax.rem(me, Z)

    def remote(src, dst, ss, rs, **where):
        return pltpu.make_async_remote_copy(
            src_ref=src, dst_ref=dst, send_sem=ss, recv_sem=rs,
            device_id=where, device_id_type=MESH,
        )

    def narrow_at(k):
        return lax.rem(mn + k, N)

    get_cent = pltpu.make_async_copy(cent_ref, cent_b, local_sem.at[0])
    get_child = pltpu.make_async_copy(child_ref, child_v, local_sem.at[1])
    get_cent.start()
    get_child.start()
    barrier = pltpu.get_barrier_semaphore()

    @pl.loop(1, W)
    def _(k):
        pl.semaphore_signal(
            barrier, inc=1, device_id={"wide": at_offset(me, k)}, device_id_type=MESH
        )

    @pl.loop(1, N)
    def _(k):
        pl.semaphore_signal(
            barrier, inc=1, device_id={"narrow": narrow_at(k)}, device_id_type=MESH
        )

    cols = pl.ds(pl.multiple_of(mn * F, F), F)
    own_rows = pl.ds(pl.multiple_of(mn * 2 * RB, 2 * RB), 2 * RB)
    pl.semaphore_wait(barrier, W - 1 + N - 1)

    def ids_copy(k):
        return remote(
            ids_ref, ids_all.at[me], ids_ss.at[k], ids_rs.at[k], wide=at_offset(me, k)
        )

    @pl.loop(1, W)
    def _(k):
        ids_copy(k).start()

    ids_all[me] = ids_ref[...]

    def e_copy(k):
        to = narrow_at(k)
        return remote(
            emb_ref.at[pl.ds(pl.multiple_of(to * 2 * RB, 2 * RB), 2 * RB)],
            xfull.at[:, cols], e_ss.at[k], e_rs.at[k], narrow=to,
        )

    @pl.loop(1, N)
    def _(k):
        e_copy(k).start()

    own_x = pltpu.make_async_copy(emb_ref.at[own_rows], xfull.at[:, cols], local_sem.at[2])
    own_x.start()
    get_cent.wait()

    @pl.loop(0, CW // 256)
    def _(i):
        rows = pl.ds(pl.multiple_of(i * 256, 256), 256)
        cent_f[rows, :] = cent_b[rows, :].astype(jnp.float32)

    @pl.loop(1, W)
    def _(k):
        ids_copy(k).wait()

    lane = lax.broadcasted_iota(jnp.int32, (W, 128), 1)
    asked = jnp.max(ids_all[...], axis=1)
    in0, in1, _ = first_two((asked >> 9) == me, lane)
    c0 = jnp.sum(jnp.where(lane == in0, asked - me * GW, 0), axis=1, keepdims=True)
    c1 = jnp.sum(jnp.where(lane == in1, asked - me * GW, 0), axis=1, keepdims=True)
    has0 = (in0 < BLK).astype(jnp.int32)
    has1 = (in1 < BLK).astype(jnp.int32)
    c0 = jnp.clip(c0 * has0, 0, GW - 1)
    c1 = jnp.clip(c1 * has1, 0, GW - 1)
    table = jnp.zeros((W, 128), jnp.int32)
    for i, column in ((0, c0), (1, c1), (4, has0), (5, has1)):
        table = jnp.where(lane == i, column, table)

    own_ids = jnp.broadcast_to(ids_ref[0:1, :], (W, 128))
    sub = lax.broadcasted_iota(jnp.int32, (W, 128), 0)
    b0, b1, _ = first_two((own_ids >> 9) == sub, lane)
    table = jnp.where(lane == 2, jnp.where(b0 < BLK, b0, 0), table)
    table = jnp.where(lane == 3, jnp.where(b1 < BLK, b1, 0), table)
    tab_out[0:W, :] = table

    lane8 = lax.broadcasted_iota(jnp.int32, (8, 128), 1)
    owner = jnp.max(ids_all[pl.ds(mx * Z, Z)], axis=1) >> 9
    owner = jnp.where(lane8 < BLK, owner, -1)
    position = jnp.zeros((8, 128), jnp.int32)
    for d in range(1, BLK):
        same = (owner == pltpu.roll(owner, d, 1)) & (lane8 >= d)
        position = jnp.where(same, 1, position)
    at = jnp.clip((owner >> 3) * 2 + position, 0, 2 * X - 1)
    tab_out[OWN_AT : OWN_AT + 8, :] = at
    tab_out[MINE : MINE + 8, :] = jnp.where((owner & 7) == mz, 1, 0)
    chosen = jnp.zeros((8, 128), jnp.int32)
    for x in range(X):
        b0, b1, _ = first_two(owner == x * Z + mz, lane8)
        chosen = jnp.where(lane8 == 2 * x, jnp.where(b0 < BLK, b0, 0), chosen)
        chosen = jnp.where(lane8 == 2 * x + 1, jnp.where(b1 < BLK, b1, 0), chosen)
    tab_out[PICK : PICK + 8, :] = chosen

    hops = (mz - (jnp.broadcast_to(ids_ref[0:1, :], (8, 128)) >> 9)) & 7
    way = jnp.where(hops < 4, 1, 2)
    way = jnp.where((hops == 4) & (lane8 < BLK // 2), 1, way)
    tab_out[LAST : LAST + 8, :] = jnp.where(hops == 0, 0, way)
    put_tab = pltpu.make_async_copy(tab_out, tab_s, local_sem.at[3])
    put_tab.start()
    put_tab.wait()
    get_child.wait()

    @pl.loop(0, W)
    def _(s):
        for j in range(2):
            row = jnp.clip(child_v[pl.ds(tab_s[s, j], 1), :] - me * CW, 0, CW - 1)
            kids_out[pl.ds(2 * s + j, 1), :] = row

    put_kids = pltpu.make_async_copy(kids_out, kids_s, local_sem.at[4])
    put_kids.start()
    put_kids.wait()

    def gather(p, dst):
        for j in range(2):

            @pl.loop(0, CH // 16)
            def _(g):
                base = pl.multiple_of(g * 16, 16)
                rows = [
                    cent_f[pl.ds(kids_s[2 * p + j, base + i], 1), :] for i in range(16)
                ]
                for i in range(16):
                    stage[j, pl.ds(base + i, 1), :] = rows[i]

        for j in range(2):
            dst[j] = stage[j].astype(jnp.bfloat16)

    def down_copy(dx, dz):
        return remote(
            x_send.at[dz, lax.rem(mx + dx, X)], x_recv[dz].at[pl.ds(2 * mx, 2)],
            d_ss.at[dx * Z + dz], d_rs.at[dx * Z + dz], wide=shifted(me, dx, 0),
        )

    def gather_for(dz):
        zs = lax.rem(mz + dz, Z)

        @pl.loop(1, X)
        def _(dx):
            xs = lax.rem(mx + dx, X)
            gather(xs * Z + zs, x_send.at[dz, xs])
            down_copy(dx, dz).start()

        gather(mx * Z + zs, x_recv[dz].at[pl.ds(2 * mx, 2)])

    def have_children(dz):
        @pl.loop(1, X)
        def _(dx):
            down_copy(dx, dz).wait()

    def down_hop(way, d, c):
        part = pl.ds(4 * c, 4)
        k = (way * 4 + d - 1) * 4 + c
        return remote(
            hop_send.at[way, d - 1, part], hop_recv.at[way, d - 1, part],
            h_ss.at[k], h_rs.at[k], wide=shifted(me, 0, 1 if way == 0 else Z - 1),
        )

    def down_parts(way, d):
        return range(4) if d < 4 else (0, 1) if way == 0 else (2, 3)

    def put_in(d):
        for dz in (d, Z - d) if d < 4 else (4,):
            have_children(dz)
        for c in range(4):
            for way in range(2):
                if c not in down_parts(way, d):
                    continue
                comes = d < 4 and c in down_parts(way, d + 1)
                if comes:
                    down_hop(way, d + 1, c).wait_recv()
                dz = d if way == 0 else Z - d
                zs = lax.rem(mz + dz, Z)

                @pl.loop(0, 4)
                def _(i):
                    b = 4 * c + i
                    value = x_recv[dz][tab_s[OWN_AT + zs, b]]
                    if comes:
                        came = hop_recv[way, d, b]
                        value = jnp.where(tab_s[MINE + zs, b] > 0, value, came)
                    hop_send[way, d - 1, b] = value

                down_hop(way, d, c).start()

    gather_for(4)
    gather_for(3)
    put_in(4)
    gather_for(5)
    gather_for(2)
    gather_for(6)
    put_in(3)
    gather_for(1)
    gather_for(7)
    put_in(2)
    gather_for(0)

    kids = kids_out[...]
    lane64 = lax.broadcasted_iota(jnp.int32, (2 * W, CH), 1)
    twice = jnp.zeros((2 * W, CH), jnp.int32)
    for d in range(1, 16):
        same = (kids == pltpu.roll(kids, d, 1)) & (lax.rem(lane64, 16) >= d)
        twice = jnp.where(same, 1, twice)
    any_twice = jnp.max(twice, axis=1, keepdims=True)
    for d in (1, 2, 4, 8):
        twice = jnp.maximum(twice, pltpu.roll(twice, CH - d, 1))
    dup_out[...] = jnp.where(lane64 == 1, any_twice, twice)

    put_in(1)
    have_children(0)
    own_x.wait()

    @pl.loop(1, N)
    def _(k):
        e_copy(k).wait()

    eye = lax.broadcasted_iota(jnp.int32, (CH, CH), 0) == lax.broadcasted_iota(
        jnp.int32, (CH, CH), 1
    )

    def as_row(column):
        return jnp.sum(jnp.where(eye, column, 0.0), axis=0, keepdims=True)

    row8 = lax.broadcasted_iota(jnp.int32, (8, CH), 0)

    def c_copy(to, sender):
        return remote(
            csel.at[pl.ds(2 * to, 2)], ctab.at[:, :, cols], c_ss.at[to], c_rs.at[sender],
            narrow=to,
        )

    def s_copy(to, sender):
        return remote(
            qsend.at[to], qrecv.at[pl.ds(2 * mn, 2)], s_ss.at[to], s_rs.at[sender], narrow=to
        )

    def t_copy(to, sender):
        return remote(
            scs.at[to], scr.at[pl.ds(2 * mn, 2)], t_ss.at[to], t_rs.at[sender], narrow=to
        )

    def weigh():
        for j in range(2):
            x = xfull[j * RB : (j + 1) * RB, :]
            squares = jnp.zeros((CH, F), jnp.float32)
            for n in range(N):
                part = ctab[j, :, n * F : (n + 1) * F].astype(jnp.float32)
                squares = squares + part * part
            lengths = as_row(jnp.sum(squares, axis=1, keepdims=True))
            dots = lax.dot_general(x, ctab[j], NT, preferred_element_type=jnp.float32)
            score = (2.0 * dots - lengths) * (1.0 / math.sqrt(D))
            e = jnp.exp(score - jnp.max(score, axis=1, keepdims=True))
            weights = (e / jnp.sum(e, axis=1, keepdims=True)).astype(jnp.bfloat16)
            weights_f = weights.astype(jnp.float32)
            counts = jnp.sum(weights_f, axis=0, keepdims=True)
            turned = weights_f.T.astype(jnp.bfloat16)
            swork[j] = jnp.dot(turned, x, preferred_element_type=jnp.float32)
            for n in range(N):
                part = swork[j, :, n * F : (n + 1) * F]
                top = jnp.maximum(jnp.max(jnp.abs(part), axis=1, keepdims=True), 1e-30)
                coded = jnp.round(part * (32767.0 / top)).astype(jnp.int32)
                qsend[n, j] = coded.astype(jnp.int16)
                scales = as_row(top * (1.0 / 32767.0))
                tile = jnp.where((row8 == 0) | (row8 == 4), scales, 0.0)
                scs[n, j] = jnp.where((row8 == 1) | (row8 == 5), counts, tile)

    @pl.loop(0, 4)
    def _(c):
        for way in range(2):
            down_hop(way, 1, c).wait_recv()

        @pl.loop(0, 4)
        def _(i):
            b = 4 * c + i
            comes = tab_s[LAST, b]
            value = jnp.where(comes == 1, hop_recv[0, 0, b], hop_recv[1, 0, b])
            csel[b] = jnp.where(comes == 0, x_recv[0][tab_s[OWN_AT + mz, b]], value)

        for i in range(2):
            to = 2 * c + i

            @pl.when(mn != to)
            def _():
                c_copy(to, mn).start()

            @pl.when(mn == to)
            def _():
                for j in range(2):
                    ctab[j, :, cols] = csel[2 * mn + j]

        @pl.when(mn // 2 == c)
        def _():
            @pl.loop(1, N)
            def _(k):
                c_copy(narrow_at(k), narrow_at(k)).wait_recv()

            weigh()

            @pl.loop(1, N)
            def _(k):
                s_copy(narrow_at(k), mn).start()
                t_copy(narrow_at(k), mn).start()

            for j in range(2):
                qrecv[2 * mn + j] = qsend[mn, j]
                scr[2 * mn + j] = scs[mn, j]

    def up_hop(way, t, c):
        part = pl.ds(4 * c, 4)
        k = (way * 4 + t - 1) * 4 + c
        src = (qrecv if t == 1 else rings[way][t - 2]).at[part]
        dst = rings[way][t - 1].at[part]
        return remote(
            src, dst, g_ss.at[k], g_rs.at[k], wide=shifted(me, 0, 1 if way == 0 else Z - 1)
        )

    def up_copy(dx, zs):
        return remote(
            pick.at[zs, lax.rem(mx + dx, X)], q_out.at[mx * Z + zs],
            u_ss.at[dx * Z + zs], u_rs.at[dx * Z + zs], wide=shifted(me, dx, 0),
        )

    def own_copy(zs):
        return pltpu.make_async_copy(pick.at[zs, mx], q_out.at[mx * Z + zs], own_sem.at[zs])

    def send_picked(zs, src):
        @pl.loop(1, X)
        def _(dx):
            xs = lax.rem(mx + dx, X)
            for j in range(2):
                pick[zs, xs, j] = src[tab_s[PICK + zs, 2 * xs + j]]
            up_copy(dx, zs).start()

        for j in range(2):
            pick[zs, mx, j] = src[tab_s[PICK + zs, 2 * mx + j]]
        own_copy(zs).start()

    @pl.loop(0, 4)
    def _(c):
        for i in range(2):
            sender = 2 * c + i

            @pl.when(mn != sender)
            def _():
                s_copy(sender, sender).wait_recv()
                t_copy(sender, sender).wait_recv()

        up_hop(0, 1, c).start()
        up_hop(1, 1, c).start()

    def scale_copy(k):
        to = at_offset(me, k)
        return remote(scu.at[to], sc_out.at[me], v_ss.at[k], v_rs.at[k], wide=to)

    def fill_scale(p):
        return jnp.where(row8 < 4, scr[tab_s[p, 2]], scr[tab_s[p, 3]])

    @pl.loop(1, W)
    def _(k):
        p = at_offset(me, k)
        scu[p] = fill_scale(p)
        scale_copy(k).start()

    sc_out[me] = fill_scale(me)
    send_picked(mz, qrecv)

    square_sub = lax.broadcasted_iota(jnp.int32, (CH, CH), 0)
    counts_v[...] = jnp.zeros_like(counts_v)

    def count(first, end):
        @pl.loop(first, end)
        def _(s):
            tile = sc_out[s]
            total = jnp.zeros((CH, CH), jnp.float32)
            for j in range(2):
                kid = kids_out[pl.ds(2 * s + j, 1), :]
                row = jnp.where(tab_s[s, 4 + j] > 0, tile[4 * j + 1 : 4 * j + 2, :], 0.0)
                low = ((kid & 127) == square_sub).astype(jnp.bfloat16)
                left = jnp.where((kid >> 7) == square_sub, row, 0.0)
                for _ in range(3):
                    piece = left.astype(jnp.bfloat16)
                    total = total + lax.dot_general(
                        low, piece, NT, preferred_element_type=jnp.float32
                    )
                    left = left - piece.astype(jnp.float32)
            counts_v[...] += total

    def pass_on(t):
        for c in range(4):
            for way in range(2):
                up_hop(way, t, c).wait_recv()
                if t < 3 or c in down_parts(way, 4):
                    up_hop(way, t + 1, c).start()
        for way in range(2):
            send_picked(lax.rem(mz + (Z - t if way == 0 else t), Z), rings[way][t - 1])

    pass_on(1)

    @pl.loop(1, W)
    def _(k):
        scale_copy(k).wait()

    count(0, W // 2)
    pass_on(2)
    count(W // 2, W)
    factor_out[...] = 1.0 / (counts_v[...] + 1.0)
    pass_on(3)
    for way in range(2):
        for c in down_parts(way, 4):
            up_hop(way, 4, c).wait_recv()
    send_picked(lax.rem(mz + 4, Z), rings[0][3])

    for way in range(2):
        for d in range(1, 5):
            for c in down_parts(way, d):
                down_hop(way, d, c).wait_send()
                up_hop(way, d, c).wait_send()

    @pl.loop(1, N)
    def _(k):
        c_copy(narrow_at(k), mn).wait_send()
        s_copy(narrow_at(k), mn).wait_send()
        t_copy(narrow_at(k), mn).wait_send()

    @pl.loop(0, Z)
    def _(zs):
        @pl.loop(1, X)
        def _(dx):
            up_copy(dx, zs).wait()

        own_copy(zs).wait()


def exchange(ids, children, centroids, embeddings):
    vm = pl.BlockSpec(memory_space=pltpu.VMEM)
    hbm = pl.BlockSpec(memory_space=pl.ANY)
    dma = pltpu.SemaphoreType.DMA
    bf, f32, i32, i16 = jnp.bfloat16, jnp.float32, jnp.int32, jnp.int16
    return pl.pallas_call(
        exchange_kernel,
        out_shape=(
            jax.ShapeDtypeStruct((W, 2, CH, F), i16),
            jax.ShapeDtypeStruct((W, 8, CH), f32),
            jax.ShapeDtypeStruct((2 * W, CH), i32),
            jax.ShapeDtypeStruct((ROWS, 128), i32),
            jax.ShapeDtypeStruct((2 * W, CH), i32),
            jax.ShapeDtypeStruct((CH, CH), f32),
        ),
        in_specs=[vm, hbm, hbm, hbm],
        out_specs=(hbm, vm, vm, vm, vm, vm),
        scratch_shapes=[
            pltpu.VMEM((W, 8, 128), i32),
            pltpu.SMEM((ROWS, 128), i32),
            pltpu.SMEM((2 * W, CH), i32),
            pltpu.VMEM((CW, F), bf),
            pltpu.VMEM((GW, CH), i32),
            pltpu.VMEM((CW, F), f32),
            pltpu.VMEM((2, CH, F), f32),
            pltpu.VMEM((CH, CH), f32),
            pltpu.VMEM((Z, X, 2, CH, F), bf),
            pltpu.VMEM((2, 4, BLK, CH, F), bf),
            pltpu.VMEM((2, 4, BLK, CH, F), bf),
            pltpu.VMEM((2 * RB, D), bf),
            pltpu.VMEM((BLK, CH, F), bf),
            pltpu.VMEM((2, CH, D), bf),
            pltpu.VMEM((N, 2, CH, F), i16),
            pltpu.VMEM((N, 2, 8, CH), f32),
            pltpu.VMEM((BLK, CH, F), i16),
            pltpu.VMEM((BLK, 8, CH), f32),
            pltpu.VMEM((Z, X, 2, CH, F), i16),
            pltpu.VMEM((W, 8, CH), f32),
            pltpu.VMEM((2, CH, D), f32),
            dma((5,)),
            dma((W,)), dma((W,)),
            dma((N,)), dma((N,)),
            dma((W,)), dma((W,)),
            dma((32,)), dma((32,)),
            dma((N,)), dma((N,)),
            dma((N,)), dma((N,)),
            dma((N,)), dma((N,)),
            dma((W,)), dma((W,)),
            dma((32,)), dma((32,)),
            dma((W,)), dma((W,)),
            dma((Z,)),
        ]
        + [pltpu.VMEM((2 * X, CH, F), bf)] * Z
        + [pltpu.VMEM((BLK, CH, F), i16)] * 7,
        compiler_params=pltpu.CompilerParams(
            collective_id=0, has_side_effects=True, vmem_limit_bytes=60 * 1024 * 1024
        ),
        name="exchange",
    )(ids, children, centroids, embeddings)


PARTS = 8
BATCH = 16


def scatter_kernel(
    kids_s, tab_s, dup_s, q_hbm, sc_ref, factor_ref, cent_hbm, out_hbm,
    q_ref, cent_b, slots, acc, cent_sem, q_sem, out_sem,
):
    lane = lax.broadcasted_iota(jnp.int32, (CH, CH), 1)
    eye = lane == lax.broadcasted_iota(jnp.int32, (CH, CH), 0)
    per, rows_per = W // PARTS, CW // PARTS

    def cent_copy(i):
        rows = pl.ds(pl.multiple_of(i * rows_per, rows_per), rows_per)
        return pltpu.make_async_copy(cent_hbm.at[rows], cent_b.at[rows], cent_sem.at[i])

    def q_copy(i):
        rows = pl.ds(i * per, per)
        return pltpu.make_async_copy(q_hbm.at[rows], q_ref.at[rows], q_sem.at[i])

    def out_copy(i):
        rows = pl.ds(pl.multiple_of(i * rows_per, rows_per), rows_per)
        return pltpu.make_async_copy(acc.at[rows], out_hbm.at[rows], out_sem.at[i])

    @pl.loop(0, PARTS)
    def _(i):
        cent_copy(i).start()

    @pl.loop(0, PARTS)
    def _(i):
        q_copy(i).start()

    @pl.loop(0, PARTS)
    def _(i):
        cent_copy(i).wait()
        for t in range(4):
            step = rows_per // 4
            rows = pl.ds(pl.multiple_of(i * rows_per + t * step, step), step)
            acc[rows, :] = cent_b[rows, :].astype(jnp.float32)

    def add_batch(slot, base):
        at = [pl.ds(kids_s[slot, base + i], 1) for i in range(BATCH)]
        sums = [acc[at[i], :] + slots[slot, pl.ds(base + i, 1), :] for i in range(BATCH)]
        for i in range(BATCH):
            acc[at[i], :] = sums[i]

    def decode(s):
        tile = sc_ref[s]
        for j in range(2):
            scale = jnp.sum(
                jnp.where(eye, tile[4 * j : 4 * j + 1, :], 0.0), axis=1, keepdims=True
            )
            slots[2 * s + j] = q_ref[s, j].astype(jnp.int32).astype(jnp.float32) * scale

    def add_slot(slot):
        @pl.when(dup_s[slot, 1] == 0)
        def _():
            for g in range(CH // BATCH):
                add_batch(slot, g * BATCH)

        @pl.when(dup_s[slot, 1] > 0)
        def _():
            @pl.loop(0, CH // BATCH)
            def _(g):
                base = pl.multiple_of(g * BATCH, BATCH)

                @pl.when(dup_s[slot, base] == 0)
                def _():
                    add_batch(slot, base)

                @pl.when(dup_s[slot, base] > 0)
                def _():
                    for i in range(BATCH):
                        at = pl.ds(kids_s[slot, base + i], 1)
                        acc[at, :] = acc[at, :] + slots[slot, pl.ds(base + i, 1), :]

    @pl.loop(0, PARTS)
    def _(i):
        q_copy(i).wait()

        @pl.loop(0, per)
        def _(t):
            decode(i * per + t)

    @pl.loop(0, W)
    def _(s):
        for j in range(2):

            @pl.when(tab_s[s, 4 + j] > 0)
            def _():
                add_slot(2 * s + j)

    factors = factor_ref[...]

    for i in range(PARTS):
        for h in range(i * (rows_per // CH), (i + 1) * (rows_per // CH)):
            rows = pl.ds(h * CH, CH)
            acc[rows, :] = acc[rows, :] * factors[:, h : h + 1]
        out_copy(i).start()

    @pl.loop(0, PARTS)
    def _(i):
        out_copy(i).wait()


def scatter(kids, table, twice, q, scales, factors, centroids):
    vm = pl.BlockSpec(memory_space=pltpu.VMEM)
    sm = pl.BlockSpec(memory_space=pltpu.SMEM)
    hbm = pl.BlockSpec(memory_space=pl.ANY)
    return pl.pallas_call(
        scatter_kernel,
        out_shape=jax.ShapeDtypeStruct((CW, F), jnp.float32),
        in_specs=[sm, sm, sm, hbm, vm, vm, hbm],
        out_specs=hbm,
        scratch_shapes=[
            pltpu.VMEM((W, 2, CH, F), jnp.int16),
            pltpu.VMEM((CW, F), jnp.bfloat16),
            pltpu.VMEM((2 * W, CH, F), jnp.float32),
            pltpu.VMEM((CW, F), jnp.float32),
            pltpu.SemaphoreType.DMA((PARTS,)),
            pltpu.SemaphoreType.DMA((PARTS,)),
            pltpu.SemaphoreType.DMA((PARTS,)),
        ],
        compiler_params=pltpu.CompilerParams(vmem_limit_bytes=60 * 1024 * 1024),
        name="scatter",
    )(kids, table, twice, q, scales, factors, centroids)


def body(embeddings, centroids, level2_cluster_index, child_lists):
    ids = jnp.pad(level2_cluster_index, (0, 128 - BLK), constant_values=-1)
    ids = jnp.broadcast_to(ids[None, :], (8, 128))
    q, scales, kids, table, twice, factors = exchange(ids, child_lists, centroids, embeddings)
    return scatter(kids, table, twice, q, scales, factors, centroids)


def solution(mesh):
    placed = (P("wide", "narrow"), P("wide", "narrow"), P("wide"), P("wide", None))
    return jax.shard_map(
        body, mesh=mesh, in_specs=placed, out_specs=P("wide", "narrow"), check_vma=False
    )
```

time: 371 us -> 185 us (0.50)
  Pallas kernels: 0 us -> 184 us
  waiting for transfers between devices: 172 us -> 0 us
  other arithmetic: 99 us -> 0 us
  local copies, waits for them, and re-layouts: 44.3 us -> 1.25 us
  starting transfers between devices: 36.4 us -> 0 us
  between operations: 13.5 us -> 0.01 us
    pallas_call x0 -> x2, Pallas kernels: none -> 184 us  [the longest x1 158 us: exchange(): pl.pallas_call(exchange_kernel, out_shape=(jax.ShapeDtypeStruct((W, 2, CH...]
    all_to_all x4 -> x0, waiting for transfers between devices: 99.6 us -> none  [the longest x1 49.1 us: body(): lax.all_to_all(sums_slots.reshape(owners, capacity, kids_count, feature_m...]
    scatter-add x2 -> x0, other arithmetic: 87.3 us -> none  [the longest x1 44 us: body(): jax.ops.segment_sum(slot_sums, flat_children, num_segments=centres_owned)]
    psum x1 -> x0, waiting for transfers between devices: 72.7 us -> none  [weigh(): total_score = lax.psum(partial_score, 'narrow')]
    all_to_all x4 -> x0, starting transfers between devices: 36.4 us -> none  [the longest x1 10.1 us: body(): lax.all_to_all(slot_ids, 'wide', split_axis=0, concat_axis=0, tiled=True)]
    gather x4 -> x0, local copies, waits for them, and re-layouts: 35.3 us -> none  [the longest x1 30.1 us: body(): centroids[children].reshape(owners, capacity, kids_count, feature_matrix)]
    div x1 -> x0, other arithmetic: 4.21 us -> none  [body(): return (sums + centroids.astype(jnp.float32)) / (counts + 1.0)[:, None]]
    scatter x2 -> x0, local copies, waits for them, and re-layouts: 4.19 us -> none  [the longest x1 2.99 us: body(): sums_slots = jnp.zeros((slots, kids_count, feature_matrix), jnp.float32)....]
  transfers between devices with their start and end apart: 5 -> 0, of which waited for: 4 -> 0; matrix products, arithmetic and copies ran while one was open for 14% -> 0% of each run, Pallas kernels for 0% -> 0%
where the time goes in v1:
time: 185 us
  Pallas kernels  184 us (99%)
    pallas_call x1, Pallas kernels, exchange(): pl.pallas_call(exchange_kernel, out_shape=(jax.ShapeDtypeStruct((W, 2, CH...  158 us
    pallas_call x1, Pallas kernels, scatter(): pl.pallas_call(scatter_kernel, out_shape=jax.ShapeDtypeStruct((CW, F), jn...  26.2 us

profile of v1, /device:TPU:95, one launch (start us, length us, event | category | flops | bytes accessed | tf_op | source)
XLA Modules:
  0.0 185.1 jit_solution(80877508093629479)
XLA Ops:
  0.0 0.7 pad.4
  0.7 0.6 broadcast_in_dim.2.ids_ref
  1.3 157.6 %exchange.1 = (s16[32,2,128,128]{3,2,1,0:T(8,128)(2,1)}, f32[32,8,128]{2,1,0:T(8,128)}, s32[64,128]{1,0:T(8,128)}, s32[64,128]{1,0:T(8,128)}, s32[64,128]{1,0:T(8,128)}, /*index=5*/f32[128,128]{1,0:T(8,128)}) custom-call(s32[8,128]{1,0:T(8,128)} %broadcast_in_dim.2.ids_ref, s32[512,128]{1,0:T(8,128)} %child_ref.1, bf16[8192,128]{1,0:T(8,128)(2,1)} %cent_hbm.1, ...), custom_call_target="tpu_custom_call" | custom-call | tf_op jit(solution)/shard_map/exchange/pallas_call | solution.py:508
  158.9 26.2 %scatter.1 = f32[8192,128]{1,0:T(8,128)} custom-call(s32[64,128]{1,0:T(8,128)} %get-tuple-element.11.kids_s, s32[64,128]{1,0:T(8,128)} %get-tuple-element.12.tab_s, s32[64,128]{1,0:T(8,128)} %get-tuple-element.13.dup_s, s16[32,2,128,128]{3,2,1,0:T(8,128)(2,1)} %get-tuple-element.14.q_hbm, f32[32,8,128]{2,1,0:T(8,128)} %get-tuple-element.15.sc_ref, ...), custom_call_target="tpu_custom_call" | custom-call | tf_op jit(solution)/shard_map/scatter/pallas_call | solution.py:673

commit v2 on v1

v2 whole, which is shorter than its diff:
```python
import functools
import math

import jax
import jax.numpy as jnp
from jax import lax
from jax.experimental import pallas as pl
from jax.experimental.pallas import tpu as pltpu
from jax.sharding import PartitionSpec as P

D = 1024
X, Z = 4, 8
W = X * Z
N = 8
RB = 256
CH = 128
F = 128
BLK = 16
GW = 512
CW = 8192
MESH = pl.DeviceIdType.MESH
NT = (((1,), (1,)), ((), ()))


def shifted(me, dx, dz):
    return lax.rem(me // Z + dx, X) * Z + lax.rem(lax.rem(me, Z) + dz, Z)


def at_offset(me, k):
    return shifted(me, k // Z, lax.rem(k, Z))


def first_two(mask, lane):
    first = jnp.min(jnp.where(mask, lane, 127), axis=1, keepdims=True)
    rest = mask & (lane != first)
    second = jnp.min(jnp.where(rest, lane, 127), axis=1, keepdims=True)
    return first, second, rest


def exchange_kernel(
    ids_ref, child_ref, cent_ref, emb_ref,
    q_out, sc_out, kids_out, tab_out, dup_out, factor_out,
    ids_all, own_v, own_s, tab_s, kids_s, emb_v, cent_b, child_v, counts_v, cent_f, stage,
    e_send, x_in, c_send, ctab, q_send, t_send, swork,
    local_sem, ids_ss, ids_rs, e_ss, e_rs, c_ss, c_rs, q_ss, q_rs, t_ss, t_rs, own_sem,
):
    me = lax.axis_index("wide")
    mn = lax.axis_index("narrow")
    mx, mz, core = me // Z, lax.rem(me, Z), lax.rem(mn, 2)
    first = lax.rem(2 * mz + 4 - mn // 2, 4)

    def remote(src, dst, ss, rs, **where):
        return pltpu.make_async_remote_copy(
            src_ref=src, dst_ref=dst, send_sem=ss, recv_sem=rs,
            device_id=where, device_id_type=MESH,
        )

    def narrow_at(k):
        return lax.rem(mn + k, N)

    def lanes_of(n):
        return pl.ds(pl.multiple_of(n * F, F), F)

    def behind(dx, dz):
        return shifted(me, X - dx, Z - dz)

    get_emb = pltpu.make_async_copy(emb_ref, emb_v, local_sem.at[0])
    get_cent = pltpu.make_async_copy(cent_ref, cent_b, local_sem.at[1])
    get_child = pltpu.make_async_copy(child_ref, child_v, local_sem.at[2])
    get_emb.start()
    get_cent.start()
    get_child.start()
    barrier = pltpu.get_barrier_semaphore()

    @pl.loop(0, 2 * X)
    def _(i):
        dx, dz = i // 2, first + 4 * lax.rem(i, 2)

        @pl.when(dx + dz > 0)
        def _():
            @pl.loop(0, N)
            def _(n):
                pl.semaphore_signal(
                    barrier, inc=1, device_id={"wide": behind(dx, dz), "narrow": n},
                    device_id_type=MESH,
                )

    @pl.loop(1, W)
    def _(k):
        pl.semaphore_signal(
            barrier, inc=1, device_id={"wide": at_offset(me, k)}, device_id_type=MESH
        )

    @pl.loop(1, N)
    def _(k):
        pl.semaphore_signal(
            barrier, inc=1, device_id={"narrow": narrow_at(k)}, device_id_type=MESH
        )

    lane = lax.broadcasted_iota(jnp.int32, (W, 128), 1)
    sub = lax.broadcasted_iota(jnp.int32, (W, 128), 0)
    own_ids = jnp.broadcast_to(ids_ref[0:1, :], (W, 128))
    b0, b1, _ = first_two((own_ids >> 9) == sub, lane)
    b0 = jnp.where(b0 < BLK, b0, 0)
    b1 = jnp.where(b1 < BLK, b1, 0)
    own_v[...] = jnp.where(lane == 0, b0, jnp.where(lane == 1, b1, 0))
    put_own = pltpu.make_async_copy(own_v, own_s, local_sem.at[3])
    put_own.start()
    put_own.wait()
    get_emb.wait()
    pl.semaphore_wait(barrier, 2 * (W - 1) + W - 1 + N - 1)

    def ids_copy(k):
        return remote(
            ids_ref, ids_all.at[me], ids_ss.at[k], ids_rs.at[k], wide=at_offset(me, k)
        )

    @pl.loop(1, W)
    def _(k):
        ids_copy(k).start()

    ids_all[me] = ids_ref[...]

    def e_copy(dx, dz, j):
        to = shifted(me, dx, dz)
        k = dx * Z + dz
        return remote(
            e_send.at[to, j], x_in.at[dx, dz // 4, :, lanes_of(mn)],
            e_ss.at[2 * k + j], e_rs.at[(2 * dx + dz // 4) * N + mn],
            wide=to, narrow=2 * lax.rem(2 * mz + dz, 4) + j,
        )

    def stays(dx, dz, j):
        return (dx == 0) & (dz == 0) & (2 * lax.rem(2 * mz, 4) + j == mn)

    def send_blocks(dx):
        @pl.loop(0, Z)
        def _(m):
            u, v = m // 2 + 1, lax.rem(m, 2)
            dz = (u * (1 - v) + (Z - u) * v) * (1 - m // (Z - 1))
            to = shifted(me, dx, dz)
            for j in range(2):
                e_send[to, j] = emb_v[own_s[to, j]]

                @pl.when(jnp.logical_not(stays(dx, dz, j)))
                def _():
                    e_copy(dx, dz, j).start()

                @pl.when(stays(dx, dz, j))
                def _():
                    x_in[0, 0, :, lanes_of(mn)] = e_send[to, j]

    def blocks_left(dx):
        @pl.loop(0, Z)
        def _(dz):
            for j in range(2):

                @pl.when(jnp.logical_not(stays(dx, dz, j)))
                def _():
                    e_copy(dx, dz, j).wait_send()

    def have_blocks(dx):
        for h in range(2):
            stayed = (dx == 0) & (first == 0) & (h == 0)

            @pl.loop(0, N)
            def _(n):
                @pl.when(jnp.logical_not(stayed & (n == mn)))
                def _():
                    remote(
                        e_send.at[0, 0], x_in.at[dx, h, :, lanes_of(n)],
                        e_ss.at[0], e_rs.at[(2 * dx + h) * N + n], narrow=narrow_at(1),
                    ).wait_recv()

    send_blocks(0)
    send_blocks(1)

    get_cent.wait()

    @pl.loop(0, CW // 256)
    def _(i):
        rows = pl.ds(pl.multiple_of(i * 256, 256), 256)
        cent_f[rows, :] = cent_b[rows, :].astype(jnp.float32)

    @pl.loop(1, W)
    def _(k):
        ids_copy(k).wait()

    asked = jnp.max(ids_all[...], axis=1)
    in0, in1, _ = first_two((asked >> 9) == me, lane)
    c0 = jnp.sum(jnp.where(lane == in0, asked - me * GW, 0), axis=1, keepdims=True)
    c1 = jnp.sum(jnp.where(lane == in1, asked - me * GW, 0), axis=1, keepdims=True)
    has0 = (in0 < BLK).astype(jnp.int32)
    has1 = (in1 < BLK).astype(jnp.int32)
    c0 = jnp.clip(c0 * has0, 0, GW - 1)
    c1 = jnp.clip(c1 * has1, 0, GW - 1)
    table = jnp.zeros((W, 128), jnp.int32)
    for i, column in ((0, c0), (1, c1), (4, has0), (5, has1)):
        table = jnp.where(lane == i, column, table)
    tab_out[...] = table
    put_tab = pltpu.make_async_copy(tab_out, tab_s, local_sem.at[4])
    put_tab.start()
    put_tab.wait()
    get_child.wait()

    @pl.loop(0, W)
    def _(s):
        for j in range(2):
            row = jnp.clip(child_v[pl.ds(tab_s[s, j], 1), :] - me * CW, 0, CW - 1)
            kids_out[pl.ds(2 * s + j, 1), :] = row

    put_kids = pltpu.make_async_copy(kids_out, kids_s, local_sem.at[5])
    put_kids.start()
    put_kids.wait()

    def gather(slot, i, dst):
        @pl.loop(0, CH // 16)
        def _(g):
            base = pl.multiple_of(g * 16, 16)
            rows = [cent_f[pl.ds(kids_s[slot, base + r], 1), :] for r in range(16)]
            for r in range(16):
                stage[i, pl.ds(base + r, 1), :] = rows[r]

        dst[...] = stage[i].astype(jnp.bfloat16)

    def c_copy(half, to, sender):
        part = pl.ds(4 * half, 4)
        return remote(
            c_send.at[to, part], ctab.at[part, :, lanes_of(sender)],
            c_ss.at[half * N + to], c_rs.at[half * N + sender], narrow=to,
        )

    def own_children(half):
        part = pl.ds(4 * half, 4)
        return pltpu.make_async_copy(
            c_send.at[mn, part], ctab.at[part, :, lanes_of(mn)], local_sem.at[6 + half]
        )

    def send_children(half):
        @pl.loop(0, N)
        def _(k):
            to = narrow_at(k)
            far = lax.rem(2 * mz + 4 - to // 2, 4)

            @pl.loop(0, 2)
            def _(i):
                dx = 2 * half + i
                for h in range(2):
                    w = behind(dx, far + 4 * h)
                    gather(2 * w + lax.rem(to, 2), h, c_send.at[to, 2 * dx + h])

            @pl.when(k > 0)
            def _():
                c_copy(half, to, mn).start()

            @pl.when(k == 0)
            def _():
                own_children(half).start()

    send_children(0)
    send_children(1)

    kids = kids_out[...]
    lane64 = lax.broadcasted_iota(jnp.int32, (2 * W, CH), 1)
    twice = jnp.zeros((2 * W, CH), jnp.int32)
    for d in range(1, 16):
        same = (kids == pltpu.roll(kids, d, 1)) & (lax.rem(lane64, 16) >= d)
        twice = jnp.where(same, 1, twice)
    any_twice = jnp.max(twice, axis=1, keepdims=True)
    for d in (1, 2, 4, 8):
        twice = jnp.maximum(twice, pltpu.roll(twice, CH - d, 1))
    dup_out[...] = jnp.where(lane64 == 1, any_twice, twice)

    square_sub = lax.broadcasted_iota(jnp.int32, (CH, CH), 0)
    eye = square_sub == lax.broadcasted_iota(jnp.int32, (CH, CH), 1)

    def as_row(column):
        return jnp.sum(jnp.where(eye, column, 0.0), axis=0, keepdims=True)

    row8 = lax.broadcasted_iota(jnp.int32, (8, CH), 0)

    def weigh(dx, h):
        slot = 2 * dx + h
        x = x_in[dx, h]
        squares = jnp.zeros((CH, F), jnp.float32)
        for n in range(N):
            part = ctab[slot, :, n * F : (n + 1) * F].astype(jnp.float32)
            squares = squares + part * part
        lengths = as_row(jnp.sum(squares, axis=1, keepdims=True))
        dots = lax.dot_general(x, ctab[slot], NT, preferred_element_type=jnp.float32)
        score = (2.0 * dots - lengths) * (1.0 / math.sqrt(D))
        e = jnp.exp(score - jnp.max(score, axis=1, keepdims=True))
        weights = (e / jnp.sum(e, axis=1, keepdims=True)).astype(jnp.bfloat16)
        weights_f = weights.astype(jnp.float32)
        counts = jnp.sum(weights_f, axis=0, keepdims=True)
        turned = weights_f.T.astype(jnp.bfloat16)
        swork[h] = jnp.dot(turned, x, preferred_element_type=jnp.float32)
        for n in range(N):
            part = swork[h, :, n * F : (n + 1) * F]
            top = jnp.maximum(jnp.max(jnp.abs(part), axis=1, keepdims=True), 1e-30)
            coded = jnp.round(part * (32767.0 / top)).astype(jnp.int32)
            q_send[slot, n] = coded.astype(jnp.int16)
            scales = as_row(top * (1.0 / 32767.0))
            t_send[slot, n] = jnp.where(row8 == 0, scales, jnp.where(row8 == 1, counts, 0.0))

    def q_copy(slot, to, w, j):
        return remote(
            q_send.at[slot, to], q_out.at[w, j],
            q_ss.at[slot * N + to], q_rs.at[2 * w + j], narrow=to,
        )

    def t_copy(slot, to, w, j):
        return remote(
            t_send.at[slot, to], sc_out.at[w, j],
            t_ss.at[slot * N + to], t_rs.at[2 * w + j], narrow=to,
        )

    def own_sums(slot, w):
        return pltpu.make_async_copy(q_send.at[slot, mn], q_out.at[w, core], own_sem.at[slot])

    def send_sums(dx, h):
        slot, w = 2 * dx + h, behind(dx, first + 4 * h)

        @pl.loop(1, N)
        def _(k):
            q_copy(slot, narrow_at(k), w, core).start()
            t_copy(slot, narrow_at(k), w, core).start()

        own_sums(slot, w).start()
        sc_out[w, core] = t_send[slot, mn]

    counts_v[...] = jnp.zeros_like(counts_v)

    def take_sums(dx):
        @pl.loop(0, Z)
        def _(dz):
            w = behind(dx, dz)
            for j in range(2):
                sender = 2 * lax.rem(2 * mz + Z - dz, 4) + j

                @pl.when(sender != mn)
                def _():
                    q_copy(0, narrow_at(1), w, j).wait_recv()
                    t_copy(0, narrow_at(1), w, j).wait_recv()

            total = jnp.zeros((CH, CH), jnp.float32)
            for j in range(2):
                kid = kids_out[pl.ds(2 * w + j, 1), :]
                row = jnp.where(tab_s[w, 4 + j] > 0, sc_out[w, j][1:2, :], 0.0)
                low = ((kid & 127) == square_sub).astype(jnp.bfloat16)
                left = jnp.where((kid >> 7) == square_sub, row, 0.0)
                for _ in range(3):
                    piece = left.astype(jnp.bfloat16)
                    total = total + lax.dot_general(
                        low, piece, NT, preferred_element_type=jnp.float32
                    )
                    left = left - piece.astype(jnp.float32)
            counts_v[...] += total

    @pl.loop(0, X)
    def _(dx):
        blocks_left(dx)

        @pl.when(dx < X - 2)
        def _():
            send_blocks(dx + 2)

        @pl.when(lax.rem(dx, 2) == 0)
        def _():
            @pl.loop(1, N)
            def _(k):
                c_copy(dx // 2, narrow_at(k), narrow_at(k)).wait_recv()

            own_children(dx // 2).wait()

        have_blocks(dx)
        for h in range(2):
            weigh(dx, h)
            send_sums(dx, h)

        @pl.when(dx > 0)
        def _():
            take_sums(dx - 1)

    take_sums(X - 1)
    factor_out[...] = 1.0 / (counts_v[...] + 1.0)

    @pl.loop(1, N)
    def _(k):
        to = narrow_at(k)
        for half in range(2):
            c_copy(half, to, mn).wait_send()

        @pl.loop(0, 2 * X)
        def _(slot):
            q_copy(slot, to, 0, 0).wait_send()
            t_copy(slot, to, 0, 0).wait_send()

    @pl.loop(0, 2 * X)
    def _(slot):
        own_sums(slot, 0).wait()


def exchange(ids, children, centroids, embeddings):
    vm = pl.BlockSpec(memory_space=pltpu.VMEM)
    hbm = pl.BlockSpec(memory_space=pl.ANY)
    dma = pltpu.SemaphoreType.DMA
    bf, f32, i32, i16 = jnp.bfloat16, jnp.float32, jnp.int32, jnp.int16
    return pl.pallas_call(
        exchange_kernel,
        out_shape=(
            jax.ShapeDtypeStruct((W, 2, CH, F), i16),
            jax.ShapeDtypeStruct((W, 2, 8, CH), f32),
            jax.ShapeDtypeStruct((2 * W, CH), i32),
            jax.ShapeDtypeStruct((W, 128), i32),
            jax.ShapeDtypeStruct((2 * W, CH), i32),
            jax.ShapeDtypeStruct((CH, CH), f32),
        ),
        in_specs=[vm, hbm, hbm, hbm],
        out_specs=(hbm, vm, vm, vm, vm, vm),
        scratch_shapes=[
            pltpu.VMEM((W, 8, 128), i32),
            pltpu.VMEM((W, 128), i32),
            pltpu.SMEM((W, 128), i32),
            pltpu.SMEM((W, 128), i32),
            pltpu.SMEM((2 * W, CH), i32),
            pltpu.VMEM((BLK, RB, F), bf),
            pltpu.VMEM((CW, F), bf),
            pltpu.VMEM((GW, CH), i32),
            pltpu.VMEM((CH, CH), f32),
            pltpu.VMEM((CW, F), f32),
            pltpu.VMEM((2, CH, F), f32),
            pltpu.VMEM((W, 2, RB, F), bf),
            pltpu.VMEM((X, 2, RB, D), bf),
            pltpu.VMEM((N, 2 * X, CH, F), bf),
            pltpu.VMEM((2 * X, CH, D), bf),
            pltpu.VMEM((2 * X, N, CH, F), i16),
            pltpu.VMEM((2 * X, N, 8, CH), f32),
            pltpu.VMEM((2, CH, D), f32),
            dma((8,)),
            dma((W,)), dma((W,)),
            dma((2 * W,)), dma((2 * W,)),
            dma((2 * N,)), dma((2 * N,)),
            dma((2 * W,)), dma((2 * W,)),
            dma((2 * W,)), dma((2 * W,)),
            dma((2 * X,)),
        ],
        compiler_params=pltpu.CompilerParams(
            collective_id=0, has_side_effects=True, vmem_limit_bytes=60 * 1024 * 1024
        ),
        name="exchange",
    )(ids, children, centroids, embeddings)


PARTS = 8
BATCH = 16


def scatter_kernel(
    kids_s, tab_s, dup_s, q_hbm, sc_ref, factor_ref, cent_hbm, out_hbm,
    q_ref, cent_b, slots, acc, cent_sem, q_sem, out_sem,
):
    lane = lax.broadcasted_iota(jnp.int32, (CH, CH), 1)
    eye = lane == lax.broadcasted_iota(jnp.int32, (CH, CH), 0)
    per, rows_per = W // PARTS, CW // PARTS

    def cent_copy(i):
        rows = pl.ds(pl.multiple_of(i * rows_per, rows_per), rows_per)
        return pltpu.make_async_copy(cent_hbm.at[rows], cent_b.at[rows], cent_sem.at[i])

    def q_copy(i):
        rows = pl.ds(i * per, per)
        return pltpu.make_async_copy(q_hbm.at[rows], q_ref.at[rows], q_sem.at[i])

    def out_copy(i):
        rows = pl.ds(pl.multiple_of(i * rows_per, rows_per), rows_per)
        return pltpu.make_async_copy(acc.at[rows], out_hbm.at[rows], out_sem.at[i])

    @pl.loop(0, PARTS)
    def _(i):
        cent_copy(i).start()

    @pl.loop(0, PARTS)
    def _(i):
        q_copy(i).start()

    @pl.loop(0, PARTS)
    def _(i):
        cent_copy(i).wait()
        for t in range(4):
            step = rows_per // 4
            rows = pl.ds(pl.multiple_of(i * rows_per + t * step, step), step)
            acc[rows, :] = cent_b[rows, :].astype(jnp.float32)

    def add_batch(slot, base):
        at = [pl.ds(kids_s[slot, base + i], 1) for i in range(BATCH)]
        sums = [acc[at[i], :] + slots[slot, pl.ds(base + i, 1), :] for i in range(BATCH)]
        for i in range(BATCH):
            acc[at[i], :] = sums[i]

    def decode(s):
        for j in range(2):
            scale = jnp.sum(
                jnp.where(eye, sc_ref[s, j][0:1, :], 0.0), axis=1, keepdims=True
            )
            slots[2 * s + j] = q_ref[s, j].astype(jnp.int32).astype(jnp.float32) * scale

    def add_slot(slot):
        @pl.when(dup_s[slot, 1] == 0)
        def _():
            for g in range(CH // BATCH):
                add_batch(slot, g * BATCH)

        @pl.when(dup_s[slot, 1] > 0)
        def _():
            @pl.loop(0, CH // BATCH)
            def _(g):
                base = pl.multiple_of(g * BATCH, BATCH)

                @pl.when(dup_s[slot, base] == 0)
                def _():
                    add_batch(slot, base)

                @pl.when(dup_s[slot, base] > 0)
                def _():
                    for i in range(BATCH):
                        at = pl.ds(kids_s[slot, base + i], 1)
                        acc[at, :] = acc[at, :] + slots[slot, pl.ds(base + i, 1), :]

    @pl.loop(0, PARTS)
    def _(i):
        q_copy(i).wait()

        @pl.loop(0, per)
        def _(t):
            decode(i * per + t)

    @pl.loop(0, W)
    def _(s):
        for j in range(2):

            @pl.when(tab_s[s, 4 + j] > 0)
            def _():
                add_slot(2 * s + j)

    factors = factor_ref[...]

    for i in range(PARTS):
        for h in range(i * (rows_per // CH), (i + 1) * (rows_per // CH)):
            rows = pl.ds(h * CH, CH)
            acc[rows, :] = acc[rows, :] * factors[:, h : h + 1]
        out_copy(i).start()

    @pl.loop(0, PARTS)
    def _(i):
        out_copy(i).wait()


def scatter(kids, table, twice, q, scales, factors, centroids):
    vm = pl.BlockSpec(memory_space=pltpu.VMEM)
    sm = pl.BlockSpec(memory_space=pltpu.SMEM)
    hbm = pl.BlockSpec(memory_space=pl.ANY)
    return pl.pallas_call(
        scatter_kernel,
        out_shape=jax.ShapeDtypeStruct((CW, F), jnp.float32),
        in_specs=[sm, sm, sm, hbm, vm, vm, hbm],
        out_specs=hbm,
        scratch_shapes=[
            pltpu.VMEM((W, 2, CH, F), jnp.int16),
            pltpu.VMEM((CW, F), jnp.bfloat16),
            pltpu.VMEM((2 * W, CH, F), jnp.float32),
            pltpu.VMEM((CW, F), jnp.float32),
            pltpu.SemaphoreType.DMA((PARTS,)),
            pltpu.SemaphoreType.DMA((PARTS,)),
            pltpu.SemaphoreType.DMA((PARTS,)),
        ],
        compiler_params=pltpu.CompilerParams(vmem_limit_bytes=60 * 1024 * 1024),
        name="scatter",
    )(kids, table, twice, q, scales, factors, centroids)


def body(embeddings, centroids, level2_cluster_index, child_lists):
    ids = jnp.pad(level2_cluster_index, (0, 128 - BLK), constant_values=-1)
    ids = jnp.broadcast_to(ids[None, :], (8, 128))
    q, scales, kids, table, twice, factors = exchange(
        ids, child_lists, centroids, embeddings.reshape(BLK, RB, F)
    )
    return scatter(kids, table, twice, q, scales, factors, centroids)


def solution(mesh):
    placed = (P("wide", "narrow"), P("wide", "narrow"), P("wide"), P("wide", None))
    return jax.shard_map(
        body, mesh=mesh, in_specs=placed, out_specs=P("wide", "narrow"), check_vma=False
    )
```

time: 185 us -> 163 us (0.88)
  the two profiles are of different devices: /device:TPU:95 before, /device:TPU:51 now
where the time goes in v2:
time: 163 us
  Pallas kernels  161 us (99%)
    pallas_call x1, Pallas kernels, exchange(): pl.pallas_call(exchange_kernel, out_shape=(jax.ShapeDtypeStruct((W, 2, CH...  134 us
    pallas_call x1, Pallas kernels, scatter(): pl.pallas_call(scatter_kernel, out_shape=jax.ShapeDtypeStruct((CW, F), jn...  27.3 us

profile of v2, /device:TPU:51, one launch (start us, length us, event | category | flops | bytes accessed | tf_op | source)
XLA Modules:
  0.0 162.6 jit_solution(16671854090632899886)
XLA Ops:
  0.0 0.7 pad.4
  0.7 0.6 broadcast_in_dim.2.ids_ref
  1.3 134.0 %exchange.1 = (s16[32,2,128,128]{3,2,1,0:T(8,128)(2,1)}, f32[32,2,8,128]{3,2,1,0:T(8,128)}, s32[64,128]{1,0:T(8,128)}, s32[32,128]{1,0:T(8,128)}, s32[64,128]{1,0:T(8,128)}, /*index=5*/f32[128,128]{1,0:T(8,128)}) custom-call(s32[8,128]{1,0:T(8,128)} %broadcast_in_dim.2.ids_ref, s32[512,128]{1,0:T(8,128)} %child_ref.1, bf16[8192,128]{1,0:T(8,128)(2,1)} %cent_hbm.1, ...), custom_call_target="tpu_custom_call" | custom-call | tf_op jit(solution)/shard_map/exchange/pallas_call | solution.py:409
  135.2 27.3 %scatter.1 = f32[8192,128]{1,0:T(8,128)} custom-call(s32[64,128]{1,0:T(8,128)} %get-tuple-element.11.kids_s, s32[32,128]{1,0:T(8,128)} %get-tuple-element.12.tab_s, s32[64,128]{1,0:T(8,128)} %get-tuple-element.13.dup_s, s16[32,2,128,128]{3,2,1,0:T(8,128)(2,1)} %get-tuple-element.14.q_hbm, f32[32,2,8,128]{3,2,1,0:T(8,128)} %get-tuple-element.15.sc_ref, ...), custom_call_target="tpu_custom_call" | custom-call | tf_op jit(solution)/shard_map/scatter/pallas_call | solution.py:563

commit v3 on v2

--- a/solution.py
+++ b/solution.py
@@ -159,18 +159,17 @@
                 def _():
                     e_copy(dx, dz, j).wait_send()
 
-    def have_blocks(dx):
-        for h in range(2):
-            stayed = (dx == 0) & (first == 0) & (h == 0)
-
-            @pl.loop(0, N)
-            def _(n):
-                @pl.when(jnp.logical_not(stayed & (n == mn)))
-                def _():
-                    remote(
-                        e_send.at[0, 0], x_in.at[dx, h, :, lanes_of(n)],
-                        e_ss.at[0], e_rs.at[(2 * dx + h) * N + n], narrow=narrow_at(1),
-                    ).wait_recv()
+    def have_blocks(dx, h):
+        stayed = (dx == 0) & (first == 0) & (h == 0)
+
+        @pl.loop(0, N)
+        def _(n):
+            @pl.when(jnp.logical_not(stayed & (n == mn)))
+            def _():
+                remote(
+                    e_send.at[0, 0], x_in.at[dx, h, :, lanes_of(n)],
+                    e_ss.at[0], e_rs.at[(2 * dx + h) * N + n], narrow=narrow_at(1),
+                ).wait_recv()
 
     send_blocks(0)
     send_blocks(1)
@@ -286,15 +285,13 @@
         for n in range(N):
             part = ctab[slot, :, n * F : (n + 1) * F].astype(jnp.float32)
             squares = squares + part * part
-        lengths = as_row(jnp.sum(squares, axis=1, keepdims=True))
-        dots = lax.dot_general(x, ctab[slot], NT, preferred_element_type=jnp.float32)
+        lengths = jnp.sum(squares, axis=1, keepdims=True)
+        dots = lax.dot_general(ctab[slot], x, NT, preferred_element_type=jnp.float32)
         score = (2.0 * dots - lengths) * (1.0 / math.sqrt(D))
-        e = jnp.exp(score - jnp.max(score, axis=1, keepdims=True))
-        weights = (e / jnp.sum(e, axis=1, keepdims=True)).astype(jnp.bfloat16)
-        weights_f = weights.astype(jnp.float32)
-        counts = jnp.sum(weights_f, axis=0, keepdims=True)
-        turned = weights_f.T.astype(jnp.bfloat16)
-        swork[h] = jnp.dot(turned, x, preferred_element_type=jnp.float32)
+        e = jnp.exp(score - jnp.max(score, axis=0, keepdims=True))
+        weights = (e / jnp.sum(e, axis=0, keepdims=True)).astype(jnp.bfloat16)
+        counts = as_row(jnp.sum(weights.astype(jnp.float32), axis=1, keepdims=True))
+        swork[h] = jnp.dot(weights, x, preferred_element_type=jnp.float32)
         for n in range(N):
             part = swork[h, :, n * F : (n + 1) * F]
             top = jnp.maximum(jnp.max(jnp.abs(part), axis=1, keepdims=True), 1e-30)
@@ -329,6 +326,7 @@
         own_sums(slot, w).start()
         sc_out[w, core] = t_send[slot, mn]
 
+    half_sub = lax.broadcasted_iota(jnp.int32, (CH // 2, CH), 0)
     counts_v[...] = jnp.zeros_like(counts_v)
 
     def take_sums(dx):
@@ -343,26 +341,29 @@
                     q_copy(0, narrow_at(1), w, j).wait_recv()
                     t_copy(0, narrow_at(1), w, j).wait_recv()
 
-            total = jnp.zeros((CH, CH), jnp.float32)
+            lows, lefts = [], []
             for j in range(2):
                 kid = kids_out[pl.ds(2 * w + j, 1), :]
                 row = jnp.where(tab_s[w, 4 + j] > 0, sc_out[w, j][1:2, :], 0.0)
-                low = ((kid & 127) == square_sub).astype(jnp.bfloat16)
-                left = jnp.where((kid >> 7) == square_sub, row, 0.0)
+                lows.append(((kid & 127) == square_sub).astype(jnp.bfloat16))
+                left = jnp.where((kid >> 7) == half_sub, row, 0.0)
+                pieces = []
                 for _ in range(3):
-                    piece = left.astype(jnp.bfloat16)
-                    total = total + lax.dot_general(
-                        low, piece, NT, preferred_element_type=jnp.float32
-                    )
-                    left = left - piece.astype(jnp.float32)
+                    pieces.append(left.astype(jnp.bfloat16))
+                    left = left - pieces[-1].astype(jnp.float32)
+                pieces.append(jnp.zeros((CH // 2, CH), jnp.bfloat16))
+                lefts.append(jnp.concatenate(pieces, axis=0))
+            total = lax.dot_general(
+                jnp.concatenate(lows, axis=1), jnp.concatenate(lefts, axis=1), NT,
+                preferred_element_type=jnp.float32,
+            )
             counts_v[...] += total
 
     @pl.loop(0, X)
     def _(dx):
-        blocks_left(dx)
-
         @pl.when(dx < X - 2)
         def _():
+            blocks_left(dx)
             send_blocks(dx + 2)
 
         @pl.when(lax.rem(dx, 2) == 0)
@@ -373,17 +374,18 @@
 
             own_children(dx // 2).wait()
 
-        have_blocks(dx)
         for h in range(2):
+            have_blocks(dx, h)
             weigh(dx, h)
             send_sums(dx, h)
 
-        @pl.when(dx > 0)
-        def _():
-            take_sums(dx - 1)
-
-    take_sums(X - 1)
-    factor_out[...] = 1.0 / (counts_v[...] + 1.0)
+        take_sums(dx)
+
+    counts = counts_v[...]
+    counts = counts[:, :CH] + pltpu.roll(counts[:, :CH], CH // 2, 1) + counts[:, CH:]
+    factor_out[...] = 1.0 / (counts + 1.0)
+    blocks_left(X - 2)
+    blocks_left(X - 1)
 
     @pl.loop(1, N)
     def _(k):
@@ -427,7 +429,7 @@
             pltpu.VMEM((BLK, RB, F), bf),
             pltpu.VMEM((CW, F), bf),
             pltpu.VMEM((GW, CH), i32),
-            pltpu.VMEM((CH, CH), f32),
+            pltpu.VMEM((CH, 2 * CH), f32),
             pltpu.VMEM((CW, F), f32),
             pltpu.VMEM((2, CH, F), f32),
             pltpu.VMEM((W, 2, RB, F), bf),
@@ -531,8 +533,7 @@
     def _(i):
         q_copy(i).wait()
 
-        @pl.loop(0, per)
-        def _(t):
+        for t in range(per):
             decode(i * per + t)
 
     @pl.loop(0, W)

time: 163 us -> 159 us (0.975)
  the two profiles are of different devices: /device:TPU:51 before, /device:TPU:47 now
where the time goes in v3:
time: 159 us; the launch traced here: 158 us
  Pallas kernels  157 us (99%)
    pallas_call x1, Pallas kernels, exchange(): pl.pallas_call(exchange_kernel, out_shape=(jax.ShapeDtypeStruct((W, 2, CH...  134 us
    pallas_call x1, Pallas kernels, scatter(): pl.pallas_call(scatter_kernel, out_shape=jax.ShapeDtypeStruct((CW, F), jn...  23.2 us

profile of v3, /device:TPU:47, one launch (start us, length us, event | category | flops | bytes accessed | tf_op | source)
XLA Modules:
  0.0 158.4 jit_solution(8559021278570074084)
XLA Ops:
  0.0 0.7 pad.4
  0.7 0.6 broadcast_in_dim.2.ids_ref
  1.3 133.9 %exchange.1 = (s16[32,2,128,128]{3,2,1,0:T(8,128)(2,1)}, f32[32,2,8,128]{3,2,1,0:T(8,128)}, s32[64,128]{1,0:T(8,128)}, s32[32,128]{1,0:T(8,128)}, s32[64,128]{1,0:T(8,128)}, /*index=5*/f32[128,128]{1,0:T(8,128)}) custom-call(s32[8,128]{1,0:T(8,128)} %broadcast_in_dim.2.ids_ref, s32[512,128]{1,0:T(8,128)} %child_ref.1, bf16[8192,128]{1,0:T(8,128)(2,1)} %cent_hbm.1, ...), custom_call_target="tpu_custom_call" | custom-call | tf_op jit(solution)/shard_map/exchange/pallas_call | solution.py:411
  135.2 23.2 %scatter.1 = f32[8192,128]{1,0:T(8,128)} custom-call(s32[64,128]{1,0:T(8,128)} %get-tuple-element.11.kids_s, s32[32,128]{1,0:T(8,128)} %get-tuple-element.12.tab_s, s32[64,128]{1,0:T(8,128)} %get-tuple-element.13.dup_s, s16[32,2,128,128]{3,2,1,0:T(8,128)(2,1)} %get-tuple-element.14.q_hbm, f32[32,2,8,128]{3,2,1,0:T(8,128)} %get-tuple-element.15.sc_ref, ...), custom_call_target="tpu_custom_call" | custom-call | tf_op jit(solution)/shard_map/scatter/pallas_call | solution.py:564

commit v4 on v3

v4 whole, which is shorter than its diff:
```python
import functools
import math

import jax
import jax.numpy as jnp
from jax import lax
from jax.experimental import pallas as pl
from jax.experimental.pallas import tpu as pltpu
from jax.sharding import PartitionSpec as P

D = 1024
X, Z = 4, 8
W = X * Z
N = 8
RB = 256
CH = 128
F = 128
BLK = 16
GW = 512
CW = 8192
MESH = pl.DeviceIdType.MESH
NT = (((1,), (1,)), ((), ()))


def shifted(me, dx, dz):
    return lax.rem(me // Z + dx, X) * Z + lax.rem(lax.rem(me, Z) + dz, Z)


def at_offset(me, k):
    return shifted(me, k // Z, lax.rem(k, Z))


def split_groups(owner, lane):
    here = lane < BLK
    earlier = jnp.zeros(owner.shape, jnp.int32)
    later = jnp.zeros(owner.shape, jnp.int32)
    for d in range(1, BLK):
        earlier = jnp.where((owner == pltpu.roll(owner, d, 1)) & (lane >= d), 1, earlier)
        later = jnp.where(
            (owner == pltpu.roll(owner, 128 - d, 1)) & (lane + d < BLK), 1, later
        )

    def before(flags):
        total = flags
        for d in (1, 2, 4, 8):
            total = total + jnp.where(lane >= d, pltpu.roll(total, d, 1), 0)
        return total - flags

    head = jnp.where(here & (earlier == 0) & (later == 1), 1, 0)
    single = jnp.where(here & (earlier == 0) & (later == 0), 1, 0)
    room = BLK // 2 - jnp.sum(head, axis=1, keepdims=True)
    one = jnp.where((single == 1) & (before(single) < room), 1, head)
    two = jnp.where(here, 1 - one, 0)
    return (one == 1, two == 1), (before(one), before(two))


def exchange_kernel(
    given_ref, child_ref, cent_ref, emb_ref,
    q_out, sc_out, kids_out, tab_out, dup_out, factor_out,
    ids_ref, ids_all, own_v, own_s, tab_s, kids_s, emb_v, cent_b, child_v, counts_v, cent_f, stage,
    e_send, xfull, d_send, c_send, ctab, q_send, t_send, u_send, scu, swork,
    local_sem, ids_ss, ids_rs, e_ss, e_rs, d_ss, d_rs, c_ss, c_rs, q_ss, q_rs, t_ss, t_rs,
    u_ss, u_rs, v_ss, v_rs, own_sem, d_one, d_two, q_one, q_two, t_one, t_two,
):
    me = lax.axis_index("wide")
    mn = lax.axis_index("narrow")
    d_recv, q_recv, t_recv = (d_one, d_two), (q_one, q_two), (t_one, t_two)

    def remote(src, dst, ss, rs, **where):
        return pltpu.make_async_remote_copy(
            src_ref=src, dst_ref=dst, send_sem=ss, recv_sem=rs,
            device_id=where, device_id_type=MESH,
        )

    def narrow_at(k):
        return lax.rem(mn + k, N)

    def lanes_of(n):
        return pl.ds(pl.multiple_of(n * F, F), F)

    def wide_at(i):
        m = lax.rem(i, Z)
        u, v = m // 2 + 1, lax.rem(m, 2)
        dz = (u * (1 - v) + (Z - u) * v) * (1 - m // (Z - 1))
        return shifted(me, lax.rem(i // Z + 1, X), dz)

    get_emb = pltpu.make_async_copy(emb_ref, emb_v, local_sem.at[0])
    get_cent = pltpu.make_async_copy(cent_ref, cent_b, local_sem.at[1])
    get_child = pltpu.make_async_copy(child_ref, child_v, local_sem.at[2])
    get_emb.start()
    get_cent.start()
    get_child.start()
    ids_ref[...] = jnp.full((1, 128), -1, jnp.int32)
    ids_ref[:, 0:BLK] = given_ref[...]
    barrier = pltpu.get_barrier_semaphore()

    @pl.loop(1, W)
    def _(k):
        pl.semaphore_signal(
            barrier, inc=1, device_id={"wide": at_offset(me, k)}, device_id_type=MESH
        )

    @pl.loop(1, N)
    def _(k):
        pl.semaphore_signal(
            barrier, inc=1, device_id={"narrow": narrow_at(k)}, device_id_type=MESH
        )

    lane = lax.broadcasted_iota(jnp.int32, (W, 128), 1)
    sub = lax.broadcasted_iota(jnp.int32, (W, 128), 0)
    owner = jnp.where(lane < BLK, jnp.broadcast_to(ids_ref[...], (W, 128)) >> 9, -1)
    groups, places = split_groups(owner, lane)
    own = jnp.zeros((W, 128), jnp.int32)
    ranks = jnp.zeros((W, 128), jnp.int32)
    for g in range(2):
        mine = groups[g] & (owner == sub)
        place = jnp.sum(jnp.where(mine, places[g], 0), axis=1, keepdims=True)
        own = jnp.where(lane == g, jnp.clip(place, 0, N - 1), own)
        this = groups[g] & (places[g] + N * g == sub)
        block = jnp.sum(jnp.where(this, lane, 0), axis=1, keepdims=True)
        its = jnp.sum(jnp.where(this, owner, 0), axis=1, keepdims=True)
        ranks = jnp.where(lane == 0, ranks + block, ranks)
        ranks = jnp.where(lane == 1, ranks + its, ranks)
    own_v[0:W, :] = own
    own_v[W : 2 * W, :] = jnp.clip(ranks, 0, W - 1)
    put_own = pltpu.make_async_copy(own_v, own_s, local_sem.at[3])
    put_own.start()
    pl.semaphore_wait(barrier, W - 1 + N - 1)

    def ids_copy(k):
        return remote(
            ids_ref, ids_all.at[me], ids_ss.at[k], ids_rs.at[k], wide=at_offset(me, k)
        )

    @pl.loop(1, W)
    def _(k):
        ids_copy(k).start()

    ids_all[me] = ids_ref[...]

    put_own.wait()
    get_emb.wait()

    @pl.loop(0, BLK)
    def _(r):
        e_send[lax.rem(r, N), r // N] = emb_v[lax.rem(own_s[W + r, 0], BLK)]

    def e_copy(k):
        to = narrow_at(k)
        return remote(
            e_send.at[to], xfull.at[:, :, lanes_of(mn)], e_ss.at[k], e_rs.at[k], narrow=to
        )

    @pl.loop(1, N)
    def _(k):
        e_copy(k).start()

    own_e = pltpu.make_async_copy(e_send.at[mn], xfull.at[:, :, lanes_of(mn)], local_sem.at[0])
    own_e.start()

    get_cent.wait()

    @pl.loop(0, CW // 256)
    def _(i):
        rows = pl.ds(pl.multiple_of(i * 256, 256), 256)
        cent_f[rows, :] = cent_b[rows, :].astype(jnp.float32)

    @pl.loop(1, W)
    def _(k):
        ids_copy(k).wait()

    asked = ids_all[:, 0, :]
    owner = jnp.where(lane < BLK, asked >> 9, -1)
    groups, _ = split_groups(owner, lane)
    table = jnp.zeros((W, 128), jnp.int32)
    for g in range(2):
        mine = groups[g] & (owner == me)
        has = jnp.sum(jnp.where(mine, 1, 0), axis=1, keepdims=True)
        cluster = jnp.sum(jnp.where(mine, asked - me * GW, 0), axis=1, keepdims=True)
        table = jnp.where(lane == g, jnp.clip(cluster, 0, GW - 1), table)
        table = jnp.where(lane == 4 + g, has, table)
    tab_out[...] = table
    put_tab = pltpu.make_async_copy(tab_out, tab_s, local_sem.at[4])
    put_tab.start()
    put_tab.wait()
    get_child.wait()

    @pl.loop(0, W)
    def _(s):
        for g in range(2):
            row = jnp.clip(child_v[pl.ds(tab_s[s, g], 1), :] - me * CW, 0, CW - 1)
            kids_out[pl.ds(2 * s + g, 1), :] = row

    put_kids = pltpu.make_async_copy(kids_out, kids_s, local_sem.at[5])
    put_kids.start()
    put_kids.wait()

    def gather(g, p, dst):
        @pl.loop(0, CH // 16)
        def _(i):
            base = pl.multiple_of(i * 16, 16)
            rows = [
                cent_f[pl.ds(kids_s[2 * p + g, base + r], 1), :] for r in range(16)
            ]
            for r in range(16):
                stage[g, pl.ds(base + r, 1), :] = rows[r]

        dst[...] = stage[g].astype(jnp.bfloat16)

    def down_copy(g, i):
        to = wide_at(i)
        return remote(
            d_send.at[g, to], d_recv[g].at[me], d_ss.at[g * W + i], d_rs.at[g * W + i], wide=to
        )

    @pl.loop(0, W - 1)
    def _(i):
        gather(0, wide_at(i), d_send.at[0, wide_at(i)])
        down_copy(0, i).start()

    gather(0, me, d_one.at[me])

    @pl.loop(0, W - 1)
    def _(i):
        gather(1, wide_at(i), d_send.at[1, wide_at(i)])
        down_copy(0, i).wait_send()
        down_copy(1, i).start()

    gather(1, me, d_two.at[me])

    kids = kids_out[...]
    lane64 = lax.broadcasted_iota(jnp.int32, (2 * W, CH), 1)
    twice = jnp.zeros((2 * W, CH), jnp.int32)
    for d in range(1, 16):
        same = (kids == pltpu.roll(kids, d, 1)) & (lax.rem(lane64, 16) >= d)
        twice = jnp.where(same, 1, twice)
    any_twice = jnp.max(twice, axis=1, keepdims=True)
    for d in (1, 2, 4, 8):
        twice = jnp.maximum(twice, pltpu.roll(twice, CH - d, 1))
    dup_out[...] = jnp.where(lane64 == 1, any_twice, twice)

    own_e.wait()

    @pl.loop(1, N)
    def _(k):
        e_copy(k).wait()

    square_sub = lax.broadcasted_iota(jnp.int32, (CH, CH), 0)
    eye = square_sub == lax.broadcasted_iota(jnp.int32, (CH, CH), 1)

    def as_row(column):
        return jnp.sum(jnp.where(eye, column, 0.0), axis=0, keepdims=True)

    row4 = lax.broadcasted_iota(jnp.int32, (4, CH), 0)

    def weigh(g):
        x = xfull[g]
        squares = jnp.zeros((CH, F), jnp.float32)
        for n in range(N):
            part = ctab[g, :, n * F : (n + 1) * F].astype(jnp.float32)
            squares = squares + part * part
        lengths = jnp.sum(squares, axis=1, keepdims=True)
        dots = lax.dot_general(ctab[g], x, NT, preferred_element_type=jnp.float32)
        score = (2.0 * dots - lengths) * (1.0 / math.sqrt(D))
        e = jnp.exp(score - jnp.max(score, axis=0, keepdims=True))
        weights = (e / jnp.sum(e, axis=0, keepdims=True)).astype(jnp.bfloat16)
        counts = as_row(jnp.sum(weights.astype(jnp.float32), axis=1, keepdims=True))
        swork[...] = jnp.dot(weights, x, preferred_element_type=jnp.float32)
        for n in range(N):
            part = swork[:, n * F : (n + 1) * F]
            top = jnp.maximum(jnp.max(jnp.abs(part), axis=1, keepdims=True), 1e-30)
            coded = jnp.round(part * (32767.0 / top)).astype(jnp.int32)
            q_send[g, n] = coded.astype(jnp.int16)
            scales = as_row(top * (1.0 / 32767.0))
            t_send[g, n] = jnp.where(lax.rem(row4, 2) == 0, scales, counts)

    def c_copy(g, k):
        to = narrow_at(k)
        return remote(
            c_send.at[g, to], ctab.at[g, :, lanes_of(mn)],
            c_ss.at[g * N + k], c_rs.at[g * N + k], narrow=to,
        )

    def q_copy(g, k):
        to = narrow_at(k)
        return remote(
            q_send.at[g, to], q_recv[g].at[mn],
            q_ss.at[g * N + k], q_rs.at[g * N + k], narrow=to,
        )

    def t_copy(g, k):
        to = narrow_at(k)
        return remote(
            t_send.at[g, to], t_recv[g].at[mn],
            t_ss.at[g * N + k], t_rs.at[g * N + k], narrow=to,
        )

    def up_copy(g, i):
        to = wide_at(i)
        return remote(
            u_send.at[g, to], q_out.at[me, g], u_ss.at[g * W + i], u_rs.at[g * W + i], wide=to
        )

    def own_sums(g):
        return pltpu.make_async_copy(u_send.at[g, me], q_out.at[me, g], own_sem.at[g])

    def scale_copy(k):
        to = at_offset(me, k)
        return remote(scu.at[to], sc_out.at[me], v_ss.at[k], v_rs.at[k], wide=to)

    def scales_for(p):
        return jnp.where(row4 < 2, t_one[own_s[p, 0]], t_two[own_s[p, 1]])

    for g in range(2):

        @pl.loop(0, W - 1)
        def _(i):
            down_copy(g, i).wait_recv()

        @pl.loop(0, N)
        def _(k):
            c_send[g, narrow_at(k)] = d_recv[g][own_s[W + N * g + narrow_at(k), 1]]

            @pl.when(k > 0)
            def _():
                c_copy(g, k).start()

        ctab[g, :, lanes_of(mn)] = c_send[g, mn]

        @pl.loop(1, N)
        def _(k):
            c_copy(g, k).wait()

        weigh(g)

        @pl.loop(1, N)
        def _(k):
            q_copy(g, k).start()
            t_copy(g, k).start()

        q_recv[g][mn] = q_send[g, mn]
        t_recv[g][mn] = t_send[g, mn]

        @pl.loop(1, N)
        def _(k):
            q_copy(g, k).wait()
            t_copy(g, k).wait()

        if g == 1:

            @pl.loop(1, W)
            def _(k):
                p = at_offset(me, k)
                scu[p] = scales_for(p)
                scale_copy(k).start()

            sc_out[me] = scales_for(me)

        @pl.loop(0, W - 1)
        def _(i):
            p = wide_at(i)
            u_send[g, p] = q_recv[g][own_s[p, g]]
            up_copy(g, i).start()

        u_send[g, me] = q_recv[g][own_s[me, g]]
        own_sums(g).start()

    @pl.loop(1, W)
    def _(k):
        scale_copy(k).wait()

    half_sub = lax.broadcasted_iota(jnp.int32, (CH // 2, CH), 0)
    counts_v[...] = jnp.zeros_like(counts_v)

    @pl.loop(0, W)
    def _(w):
        tile = sc_out[w]
        lows, lefts = [], []
        for g in range(2):
            kid = kids_out[pl.ds(2 * w + g, 1), :]
            row = jnp.where(tab_s[w, 4 + g] > 0, tile[2 * g + 1 : 2 * g + 2, :], 0.0)
            lows.append(((kid & 127) == square_sub).astype(jnp.bfloat16))
            left = jnp.where((kid >> 7) == half_sub, row, 0.0)
            pieces = []
            for _ in range(3):
                pieces.append(left.astype(jnp.bfloat16))
                left = left - pieces[-1].astype(jnp.float32)
            pieces.append(jnp.zeros((CH // 2, CH), jnp.bfloat16))
            lefts.append(jnp.concatenate(pieces, axis=0))
        counts_v[...] += lax.dot_general(
            jnp.concatenate(lows, axis=1), jnp.concatenate(lefts, axis=1), NT,
            preferred_element_type=jnp.float32,
        )

    counts = counts_v[...]
    counts = counts[:, :CH] + pltpu.roll(counts[:, :CH], CH // 2, 1) + counts[:, CH:]
    factor_out[...] = 1.0 / (counts + 1.0)

    @pl.loop(0, W - 1)
    def _(i):
        down_copy(1, i).wait_send()

    for g in range(2):
        own_sums(g).wait()

        @pl.loop(0, W - 1)
        def _(i):
            up_copy(g, i).wait()


def exchange(ids, children, centroids, embeddings):
    vm = pl.BlockSpec(memory_space=pltpu.VMEM)
    hbm = pl.BlockSpec(memory_space=pl.ANY)
    dma = pltpu.SemaphoreType.DMA
    bf, f32, i32, i16 = jnp.bfloat16, jnp.float32, jnp.int32, jnp.int16
    return pl.pallas_call(
        exchange_kernel,
        out_shape=(
            jax.ShapeDtypeStruct((W, 2, CH, F), i16),
            jax.ShapeDtypeStruct((W, 4, CH), f32),
            jax.ShapeDtypeStruct((2 * W, CH), i32),
            jax.ShapeDtypeStruct((W, 128), i32),
            jax.ShapeDtypeStruct((2 * W, CH), i32),
            jax.ShapeDtypeStruct((CH, CH), f32),
        ),
        in_specs=[vm, hbm, hbm, hbm],
        out_specs=(hbm, vm, vm, vm, vm, vm),
        scratch_shapes=[
            pltpu.VMEM((1, 128), i32),
            pltpu.VMEM((W, 1, 128), i32),
            pltpu.VMEM((2 * W, 128), i32),
            pltpu.SMEM((2 * W, 128), i32),
            pltpu.SMEM((W, 128), i32),
            pltpu.SMEM((2 * W, CH), i32),
            pltpu.VMEM((BLK, RB, F), bf),
            pltpu.VMEM((CW, F), bf),
            pltpu.VMEM((GW, CH), i32),
            pltpu.VMEM((CH, 2 * CH), f32),
            pltpu.VMEM((CW, F), f32),
            pltpu.VMEM((2, CH, F), f32),
            pltpu.VMEM((N, 2, RB, F), bf),
            pltpu.VMEM((2, RB, D), bf),
            pltpu.VMEM((2, W, CH, F), bf),
            pltpu.VMEM((2, N, CH, F), bf),
            pltpu.VMEM((2, CH, D), bf),
            pltpu.VMEM((2, N, CH, F), i16),
            pltpu.VMEM((2, N, 4, CH), f32),
            pltpu.VMEM((2, W, CH, F), i16),
            pltpu.VMEM((W, 4, CH), f32),
            pltpu.VMEM((CH, D), f32),
            dma((6,)),
            dma((W,)), dma((W,)),
            dma((N,)), dma((N,)),
            dma((2 * W,)), dma((2 * W,)),
            dma((2 * N,)), dma((2 * N,)),
            dma((2 * N,)), dma((2 * N,)),
            dma((2 * N,)), dma((2 * N,)),
            dma((2 * W,)), dma((2 * W,)),
            dma((W,)), dma((W,)),
            dma((2,)),
            pltpu.VMEM((W, CH, F), bf),
            pltpu.VMEM((W, CH, F), bf),
            pltpu.VMEM((N, CH, F), i16),
            pltpu.VMEM((N, CH, F), i16),
            pltpu.VMEM((N, 4, CH), f32),
            pltpu.VMEM((N, 4, CH), f32),
        ],
        compiler_params=pltpu.CompilerParams(
            collective_id=0, has_side_effects=True, vmem_limit_bytes=60 * 1024 * 1024
        ),
        name="exchange",
    )(ids, children, centroids, embeddings)


PARTS = 8
BATCH = 16


def scatter_kernel(
    kids_s, tab_s, dup_s, q_hbm, sc_ref, factor_ref, cent_hbm, out_hbm,
    q_ref, cent_b, slots, acc, acc_two, cent_sem, q_sem, out_sem,
):
    lane = lax.broadcasted_iota(jnp.int32, (CH, CH), 1)
    eye = lane == lax.broadcasted_iota(jnp.int32, (CH, CH), 0)
    per, rows_per = W // PARTS, CW // PARTS

    def cent_copy(i):
        rows = pl.ds(pl.multiple_of(i * rows_per, rows_per), rows_per)
        return pltpu.make_async_copy(cent_hbm.at[rows], cent_b.at[rows], cent_sem.at[i])

    def q_copy(i):
        rows = pl.ds(i * per, per)
        return pltpu.make_async_copy(q_hbm.at[rows], q_ref.at[rows], q_sem.at[i])

    def out_copy(i):
        rows = pl.ds(pl.multiple_of(i * rows_per, rows_per), rows_per)
        return pltpu.make_async_copy(acc.at[rows], out_hbm.at[rows], out_sem.at[i])

    @pl.loop(0, PARTS)
    def _(i):
        cent_copy(i).start()

    @pl.loop(0, PARTS)
    def _(i):
        q_copy(i).start()

    @pl.loop(0, PARTS)
    def _(i):
        cent_copy(i).wait()
        for t in range(4):
            step = rows_per // 4
            rows = pl.ds(pl.multiple_of(i * rows_per + t * step, step), step)
            acc[rows, :] = cent_b[rows, :].astype(jnp.float32)
            acc_two[rows, :] = jnp.zeros((step, F), jnp.float32)

    def add_batch(slot, base, *into):
        rows = [(to, base + BATCH * t + i) for t, to in enumerate(into) for i in range(BATCH)]
        at = [pl.ds(kids_s[slot, r], 1) for _, r in rows]
        sums = [
            to[at[i], :] + slots[slot, pl.ds(r, 1), :] for i, (to, r) in enumerate(rows)
        ]
        for i, (to, _) in enumerate(rows):
            to[at[i], :] = sums[i]

    def decode(s):
        for j in range(2):
            scale = jnp.sum(
                jnp.where(eye, sc_ref[s][2 * j : 2 * j + 1, :], 0.0), axis=1, keepdims=True
            )
            slots[2 * s + j] = q_ref[s, j].astype(jnp.int32).astype(jnp.float32) * scale

    def add_slot(slot):
        @pl.when(dup_s[slot, 1] == 0)
        def _():
            for g in range(CH // BATCH // 2):
                add_batch(slot, 2 * g * BATCH, acc, acc_two)

        @pl.when(dup_s[slot, 1] > 0)
        def _():
            @pl.loop(0, CH // BATCH)
            def _(g):
                base = pl.multiple_of(g * BATCH, BATCH)

                @pl.when(dup_s[slot, base] == 0)
                def _():
                    add_batch(slot, base, acc)

                @pl.when(dup_s[slot, base] > 0)
                def _():
                    for i in range(BATCH):
                        at = pl.ds(kids_s[slot, base + i], 1)
                        acc[at, :] = acc[at, :] + slots[slot, pl.ds(base + i, 1), :]

    @pl.loop(0, PARTS)
    def _(i):
        q_copy(i).wait()

        for t in range(per):
            decode(i * per + t)

    @pl.loop(0, W)
    def _(s):
        for j in range(2):

            @pl.when(tab_s[s, 4 + j] > 0)
            def _():
                add_slot(2 * s + j)

    factors = factor_ref[...]

    for i in range(PARTS):
        for h in range(i * (rows_per // CH), (i + 1) * (rows_per // CH)):
            rows = pl.ds(h * CH, CH)
            acc[rows, :] = (acc[rows, :] + acc_two[rows, :]) * factors[:, h : h + 1]
        out_copy(i).start()

    @pl.loop(0, PARTS)
    def _(i):
        out_copy(i).wait()


def scatter(kids, table, twice, q, scales, factors, centroids):
    vm = pl.BlockSpec(memory_space=pltpu.VMEM)
    sm = pl.BlockSpec(memory_space=pltpu.SMEM)
    hbm = pl.BlockSpec(memory_space=pl.ANY)
    return pl.pallas_call(
        scatter_kernel,
        out_shape=jax.ShapeDtypeStruct((CW, F), jnp.float32),
        in_specs=[sm, sm, sm, hbm, vm, vm, hbm],
        out_specs=hbm,
        scratch_shapes=[
            pltpu.VMEM((W, 2, CH, F), jnp.int16),
            pltpu.VMEM((CW, F), jnp.bfloat16),
            pltpu.VMEM((2 * W, CH, F), jnp.float32),
            pltpu.VMEM((CW, F), jnp.float32),
            pltpu.VMEM((CW, F), jnp.float32),
            pltpu.SemaphoreType.DMA((PARTS,)),
            pltpu.SemaphoreType.DMA((PARTS,)),
            pltpu.SemaphoreType.DMA((PARTS,)),
        ],
        compiler_params=pltpu.CompilerParams(vmem_limit_bytes=60 * 1024 * 1024),
        name="scatter",
    )(kids, table, twice, q, scales, factors, centroids)


def body(embeddings, centroids, level2_cluster_index, child_lists):
    ids = level2_cluster_index.reshape(1, BLK)
    q, scales, kids, table, twice, factors = exchange(
        ids, child_lists, centroids, embeddings.reshape(BLK, RB, F)
    )
    return scatter(kids, table, twice, q, scales, factors, centroids)


def solution(mesh):
    placed = (P("wide", "narrow"), P("wide", "narrow"), P("wide"), P("wide", None))
    return jax.shard_map(
        body, mesh=mesh, in_specs=placed, out_specs=P("wide", "narrow"), check_vma=False
    )
```

time: 159 us -> 140 us (0.88)
  the two profiles are of different devices: /device:TPU:47 before, /device:TPU:112 now
where the time goes in v4:
time: 140 us
  Pallas kernels  140 us (100%)
    pallas_call x1, Pallas kernels, exchange(): pl.pallas_call(exchange_kernel, out_shape=(jax.ShapeDtypeStruct((W, 2, CH...  116 us
    pallas_call x1, Pallas kernels, scatter(): pl.pallas_call(scatter_kernel, out_shape=jax.ShapeDtypeStruct((CW, F), jn...  24.1 us

profile of v4, /device:TPU:112, one launch (start us, length us, event | category | flops | bytes accessed | tf_op | source)
XLA Modules:
  0.0 140.2 jit_solution(15050523203864616886)
XLA Ops:
  0.0 116.2 %exchange.1 = (s16[32,2,128,128]{3,2,1,0:T(8,128)(2,1)}, f32[32,4,128]{2,1,0:T(4,128)}, s32[64,128]{1,0:T(8,128)}, s32[32,128]{1,0:T(8,128)}, s32[64,128]{1,0:T(8,128)}, /*index=5*/f32[128,128]{1,0:T(8,128)}) custom-call(s32[1,16]{1,0:T(1,128)} %bitcast.3, s32[512,128]{1,0:T(8,128)} %child_ref.1, bf16[8192,128]{1,0:T(8,128)(2,1)} %cent_hbm.1, ...), custom_call_target="tpu_custom_call" | custom-call | tf_op jit(solution)/shard_map/exchange/pallas_call | solution.py:416
  116.2 24.1 %scatter.1 = f32[8192,128]{1,0:T(8,128)} custom-call(s32[64,128]{1,0:T(8,128)} %get-tuple-element.11.kids_s, s32[32,128]{1,0:T(8,128)} %get-tuple-element.12.tab_s, s32[64,128]{1,0:T(8,128)} %get-tuple-element.13.dup_s, s16[32,2,128,128]{3,2,1,0:T(8,128)(2,1)} %get-tuple-element.14.q_hbm, f32[32,4,128]{2,1,0:T(4,128)} %get-tuple-element.15.sc_ref, ...), custom_call_target="tpu_custom_call" | custom-call | tf_op jit(solution)/shard_map/scatter/pallas_call | solution.py:586
